TPU v7x, 512 devices: a whole 4x8x8 slice. The times are simulated.
512 devices in a mesh: dp: 4 (over z_hi), outer: 16 (over z_lo, y), inner: 8 (over x, core).
Axes of the slice: x: 4, y: 8, z: 8 (z_hi: 4, z_lo: 2; z = z_hi * 2 + z_lo), core: 2. Of those that a mesh axis runs over, the one named last changes fastest.
Arguments:
- queries: bfloat16 [4, 24576, 1024], P('dp', ('outer', 'inner')), may hold values from -6 to 6
- inputs: bfloat16 [4, 24576, 1024], P('dp', ('outer', 'inner')), may hold values from -24 to 24
- kv_weight: bfloat16 [1024, 512], replicated, may hold values from -0.1875 to 0.1875
- grad_out: bfloat16 [4, 24576, 1024], P('dp', ('outer', 'inner')), may hold values from -6 to 6
- segment_ids: int32 [4, 24576], P('dp', ('outer', 'inner')), may hold values from 0 to 63, never falling along the last dimension, each value on 1 to 768 neighbouring positions
Outputs:
- grad_queries: bfloat16 [4, 24576, 1024], P('dp', ('outer', 'inner'))
- grad_inputs: bfloat16 [4, 24576, 1024], P('dp', ('outer', 'inner'))
- grad_weight: float32 [1024, 512], P(('outer', 'inner'))
Inputs may be any that keep to these rules, and one draw needn't show every extreme that they name: `segment_ids`: along each replica's row the volume numbers never fall; every volume has 1 to 768 tokens, and some volume has exactly 768.
All inputs are finite; a program needn't handle non-finite values.
Results may differ from a plain program's by a relative error of at most 0.011.
Values may be sent and summed in bfloat16 or wider, within the bound.
A program may use at most 64 MiB of HBM per device.

v0:
```python
import jax
import jax.numpy as jnp
from jax import lax
from jax.sharding import PartitionSpec as P

HEADS = 8
KV_HEADS = 2
HEAD = 128
REACH = 4


def shifted(value, axis, steps):
    count = lax.axis_size(axis)
    leading, last = (max(0, -steps), min(count, count - steps))
    return lax.ppermute(value, axis, [(source, source + steps) for source in range(leading, last)])


def contract(left, right, left_dim, right_dim):
    return lax.dot_general(
        left, right, (((left_dim,), (right_dim,)), ((), ())), preferred_element_type=jnp.float32
    )


def attend(query_rows, upstream, window, volume_here, volume_window):
    factor = HEAD ** (-0.5)
    per_group = HEADS // KV_HEADS
    query_count = query_rows.shape[0]
    allowed = volume_here[:, None] == volume_window[None, :]
    allowed = jnp.repeat(allowed, per_group, axis=0)
    grad_query_parts = []
    key_parts = []
    value_parts = []
    for group in range(KV_HEADS):
        lo_col = group * per_group * HEAD
        hi_col = (group + 1) * per_group * HEAD
        query_group = query_rows[:, lo_col:hi_col].reshape(query_count * per_group, HEAD)
        upstream_group = upstream[:, lo_col:hi_col].reshape(query_count * per_group, HEAD)
        keys = window[:, group * HEAD : (group + 1) * HEAD]
        values = window[:, (KV_HEADS + group) * HEAD : (KV_HEADS + group + 1) * HEAD]
        scores = contract(query_group, keys, 1, 1) * factor
        scores = jnp.where(allowed, scores, -1e30)
        peak = jnp.max(scores, axis=1, keepdims=True)
        log_total = peak + jnp.log(jnp.sum(jnp.exp(scores - peak), axis=1, keepdims=True))
        probs = jnp.exp(scores - log_total)
        probs_low = probs.astype(jnp.bfloat16)
        output = jnp.dot(probs_low, values, preferred_element_type=jnp.float32)
        dot_term = jnp.sum(upstream_group.astype(jnp.float32) * output, axis=1, keepdims=True)
        grad_probs = contract(upstream_group, values, 1, 1)
        grad_scores = (probs * (grad_probs - dot_term) * factor).astype(jnp.bfloat16)
        grad_query = jnp.dot(grad_scores, keys, preferred_element_type=jnp.float32)
        grad_query_parts.append(grad_query.reshape(query_count, per_group * HEAD))
        key_parts.append(contract(grad_scores, query_group, 0, 0))
        value_parts.append(contract(probs_low, upstream_group, 0, 0))
    return (
        jnp.concatenate(grad_query_parts, axis=1),
        jnp.concatenate(key_parts + value_parts, axis=1),
    )


def fetch_direct(pair, offset):
    return shifted((pair[0], pair[1]), ("outer", "inner"), offset)


def return_direct(parcel, offset):
    return shifted(parcel, ("outer", "inner"), offset).astype(jnp.float32)


def on_device(queries, inputs, kv_weight, grad_out, segment_ids):
    query_rows = queries[0]
    input_rows = inputs[0]
    upstream = grad_out[0]
    volume_here = segment_ids[0] + 1
    tok_rows = query_rows.shape[0]
    key_value = jnp.dot(input_rows, kv_weight, preferred_element_type=jnp.float32).astype(
        jnp.bfloat16
    )
    pieces = {0: (key_value, volume_here)}
    for offset in range(1, REACH + 1):
        pieces[-offset] = fetch_direct(pieces[0], offset)
        pieces[offset] = fetch_direct(pieces[0], -offset)
    window = jnp.concatenate([pieces[offset][0] for offset in range(-REACH, REACH + 1)], axis=0)
    volume_window = jnp.concatenate(
        [pieces[offset][1] for offset in range(-REACH, REACH + 1)], axis=0
    )
    grad_query, grad_window = attend(query_rows, upstream, window, volume_here, volume_window)
    parcels = grad_window.astype(jnp.bfloat16)
    parcels = [parcels[index * tok_rows : (index + 1) * tok_rows] for index in range(2 * REACH + 1)]
    total = lax.optimization_barrier(parcels[REACH]).astype(jnp.float32)
    for offset in range(1, REACH + 1):
        total = total + return_direct(parcels[REACH - offset], -offset)
        total = total + return_direct(parcels[REACH + offset], offset)
    grad_kv = total.astype(jnp.bfloat16)
    grad_input = contract(grad_kv, kv_weight, 1, 1).astype(jnp.bfloat16)
    share = lax.psum_scatter(
        contract(input_rows, grad_kv, 0, 0), ("outer", "inner"), scatter_dimension=0, tiled=True
    )
    grad_weight = lax.psum(share, "dp")
    return (grad_query.astype(jnp.bfloat16)[None], grad_input[None], grad_weight)


def solution(mesh):
    in_specs = (
        P("dp", ("outer", "inner"), None),
        P("dp", ("outer", "inner"), None),
        P(),
        P("dp", ("outer", "inner"), None),
        P("dp", ("outer", "inner")),
    )
    out_specs = (
        P("dp", ("outer", "inner"), None),
        P("dp", ("outer", "inner"), None),
        P(("outer", "inner"), None),
    )
    return jax.shard_map(
        on_device, mesh=mesh, in_specs=in_specs, out_specs=out_specs, check_vma=False
    )
```

profile of v0, /device:TPU:1, one launch (start us, length us, event | category | flops | bytes accessed | tf_op | source)
XLA Modules:
  0.0 750.9 jit_solution(17589105465910176954)
XLA Ops:
  9.3 1.3 collective-permute-start.6
  10.6 1.3 collective-permute-start.5
  11.9 8.8 %collective-permute-start.4 = (s32[192]{0:T(256)S(1)}, s32[192]{0:T(256)S(1)}, u32[]{:S(2)}, u32[]{:S(2)}) collective-permute-start(s32[192]{0:T(256)S(1)} %bitcast.50), channel_id=1, source_target_pairs={{1,0},{2,1},{3,2},{4,3},{5,4},{6,5},{7,6},{8,7},{9,8},{10,9},{11,1... | collective-permute-start | bytes 2312 | tf_op jit(solution)/shard_map/ppermute | solution.py:15
  20.7 4.2 collective-permute-start.3
  25.9 2.1 convolution_convert_fusion.5
  28.2 4.3 collective-permute-start.2
  32.5 4.7 collective-permute-start.1
  37.3 5.6 collective-permute-start
  44.2 1.3 collective-permute-start.15
  45.5 1.3 collective-permute-start.14
  48.2 8.9 %collective-permute-start.9 = (bf16[192,512]{1,0:T(8,128)(2,1)}, bf16[192,512]{1,0:T(8,128)(2,1)}, u32[]{:S(2)}, u32[]{:S(2)}) collective-permute-start(bf16[192,512]{1,0:T(8,128)(2,1)} %convolution_convert_fusion.5), channel_id=1, source_target_pairs={{0,3},{1,4},{2,5},{3,6},{4,7},{5,8},{6,9},{7,10},{8,11},{9,12},{10... | collective-permute-start | bytes 589832 | tf_op jit(solution)/shard_map/ppermute | solution.py:15
  57.1 4.9 collective-permute-start.8
  63.5 2.8 reshape.84
  66.4 2.8 copy.14
  69.1 3.4 collective-permute-start.10
  73.5 2.4 collective-permute-start.11
  76.9 3.9 collective-permute-start.12
  81.8 4.3 collective-permute-done.12
  102.5 3.8 collective-permute-start.23
  106.2 1.3 collective-permute-start.22
  107.5 5.0 collective-permute-start.21
  112.6 1.5 collective-permute-start.20
  114.1 3.7 collective-permute-start.19
  119.1 5.2 collective-permute-start.17
  124.4 1.9 collective-permute-start.16
  126.6 1.4 collective-permute-done.18
  128.7 2.6 collective-permute-done.16
  132.1 1.8 copy.19
  134.0 2.8 convolution_convert_fusion.6
  136.9 2.7 convolution_convert_fusion.7
  141.8 579.7 %reduce-scatter.4.cloned.1.call-done = f32[8,512]{1,0:T(8,128)} async-done(((f32[1024,512]{1,0:T(8,128)}), f32[8,512]{1,0:T(8,128)}) %reduce-scatter.4.cloned.1.call-update) | async-done | bytes 16400
  722.4 20.9 %psum.7 = f32[8,512]{0,1:T(8,128)S(1)} all-reduce(f32[8,512]{0,1:T(8,128)S(1)} %copy.20), channel_id=1, replica_groups=mesh['dp'=4,'outer'=16,'inner'=8] {'dp'}, use_global_device_ids=true, to_apply=%region_7.8 | all-reduce | flops 4096 | bytes 32768 | tf_op jit(solution)/shard_map/psum | solution.py:97
  (85 shorter events, 33.5 us)
Async XLA Ops:
  7.2 18.8 %copy-start = (bf16[1024,512]{1,0:T(8,128)(2,1)S(1)}, bf16[1024,512]{1,0:T(8,128)(2,1)}, u32[]{:S(2)}) copy-start(bf16[1024,512]{1,0:T(8,128)(2,1)} %param.7) | copy-start | bytes 3145732
  7.2 20.8 %copy-start.6 = (bf16[1,192,1024]{2,1,0:T(8,128)(2,1)S(1)}, bf16[1,192,1024]{2,1,0:T(8,128)(2,1)}, u32[]{:S(2)}) copy-start(bf16[1,192,1024]{2,1,0:T(8,128)(2,1)} %param.8) | copy-start | bytes 1179652
  7.2 714.4 %reduce-scatter.4.cloned.1.call-start = ((), (), s32[]{:S(2)}) async-start(), calls=%async_computation.1 | async-start | bytes 2113536
  8.0 20.1 %collective-permute-start.7 = (s32[192]{0:T(256)S(1)}, s32[192]{0:T(256)S(1)}, u32[]{:S(2)}, u32[]{:S(2)}) collective-permute-start(s32[192]{0:T(256)S(1)} %bitcast.47), channel_id=1, source_target_pairs={{4,0},{5,1},{6,2},{7,3},{8,4},{9,5},{10,6},{11,7},{12,8},{13,9},{1... | collective-permute-start | bytes 2312 | tf_op jit(solution)/shard_map/ppermute | solution.py:15
  9.3 23.2 %collective-permute-start.6 = (s32[192]{0:T(256)S(1)}, s32[192]{0:T(256)S(1)}, u32[]{:S(2)}, u32[]{:S(2)}) collective-permute-start(s32[192]{0:T(256)S(1)} %bitcast.48), channel_id=1, source_target_pairs={{3,0},{4,1},{5,2},{6,3},{7,4},{8,5},{9,6},{10,7},{11,8},{12,9},{13... | collective-permute-start | bytes 2312 | tf_op jit(solution)/shard_map/ppermute | solution.py:15
  10.6 26.7 %collective-permute-start.5 = (s32[192]{0:T(256)S(1)}, s32[192]{0:T(256)S(1)}, u32[]{:S(2)}, u32[]{:S(2)}) collective-permute-start(s32[192]{0:T(256)S(1)} %bitcast.49), channel_id=1, source_target_pairs={{2,0},{3,1},{4,2},{5,3},{6,4},{7,5},{8,6},{9,7},{10,8},{11,9},{12,... | collective-permute-start | bytes 2312 | tf_op jit(solution)/shard_map/ppermute | solution.py:15
  11.9 32.3 %collective-permute-start.4 = (s32[192]{0:T(256)S(1)}, s32[192]{0:T(256)S(1)}, u32[]{:S(2)}, u32[]{:S(2)}) collective-permute-start(s32[192]{0:T(256)S(1)} %bitcast.50), channel_id=1, source_target_pairs={{1,0},{2,1},{3,2},{4,3},{5,4},{6,5},{7,6},{8,7},{9,8},{10,9},{11,1... | collective-permute-start | bytes 2312 | tf_op jit(solution)/shard_map/ppermute | solution.py:15
  20.7 24.8 %collective-permute-start.3 = (s32[192]{0:T(256)S(1)}, s32[192]{0:T(256)S(1)}, u32[]{:S(2)}, u32[]{:S(2)}) collective-permute-start(s32[192]{0:T(256)S(1)} %bitcast.51), channel_id=1, source_target_pairs={{0,1},{1,2},{2,3},{3,4},{4,5},{5,6},{6,7},{7,8},{8,9},{9,10},{10,1... | collective-permute-start | bytes 2312 | tf_op jit(solution)/shard_map/ppermute | solution.py:15
  28.2 18.7 %collective-permute-start.2 = (s32[192]{0:T(256)S(1)}, s32[192]{0:T(256)S(1)}, u32[]{:S(2)}, u32[]{:S(2)}) collective-permute-start(s32[192]{0:T(256)S(1)} %bitcast.52), channel_id=1, source_target_pairs={{0,2},{1,3},{2,4},{3,5},{4,6},{5,7},{6,8},{7,9},{8,10},{9,11},{10,... | collective-permute-start | bytes 2312 | tf_op jit(solution)/shard_map/ppermute | solution.py:15
  32.5 15.6 %collective-permute-start.1 = (s32[192]{0:T(256)S(1)}, s32[192]{0:T(256)S(1)}, u32[]{:S(2)}, u32[]{:S(2)}) collective-permute-start(s32[192]{0:T(256)S(1)} %bitcast.53), channel_id=1, source_target_pairs={{0,3},{1,4},{2,5},{3,6},{4,7},{5,8},{6,9},{7,10},{8,11},{9,12},{10... | collective-permute-start | bytes 2312 | tf_op jit(solution)/shard_map/ppermute | solution.py:15
  37.3 19.8 %collective-permute-start = (s32[192]{0:T(256)S(1)}, s32[192]{0:T(256)S(1)}, u32[]{:S(2)}, u32[]{:S(2)}) collective-permute-start(s32[192]{0:T(256)S(1)} %bitcast.54), channel_id=1, source_target_pairs={{0,4},{1,5},{2,6},{3,7},{4,8},{5,9},{6,10},{7,11},{8,12},{9,13},{1... | collective-permute-start | bytes 2312 | tf_op jit(solution)/shard_map/ppermute | solution.py:15
  44.2 43.8 %collective-permute-start.15 = (bf16[192,512]{1,0:T(8,128)(2,1)}, bf16[192,512]{1,0:T(8,128)(2,1)}, u32[]{:S(2)}, u32[]{:S(2)}) collective-permute-start(bf16[192,512]{1,0:T(8,128)(2,1)} %convolution_convert_fusion.5), channel_id=1, source_target_pairs={{4,0},{5,1},{6,2},{7,3},{8,4},{9,5},{10,6},{11,7},{12,8},{13,9},{1... | collective-permute-start | bytes 589832 | tf_op jit(solution)/shard_map/ppermute | solution.py:15
  45.5 41.6 %collective-permute-start.14 = (bf16[192,512]{1,0:T(8,128)(2,1)}, bf16[192,512]{1,0:T(8,128)(2,1)}, u32[]{:S(2)}, u32[]{:S(2)}) collective-permute-start(bf16[192,512]{1,0:T(8,128)(2,1)} %convolution_convert_fusion.5), channel_id=1, source_target_pairs={{3,0},{4,1},{5,2},{6,3},{7,4},{8,5},{9,6},{10,7},{11,8},{12,9},{13... | collective-permute-start | bytes 589832 | tf_op jit(solution)/shard_map/ppermute | solution.py:15
  46.9 39.3 %collective-permute-start.13 = (bf16[192,512]{1,0:T(8,128)(2,1)}, bf16[192,512]{1,0:T(8,128)(2,1)}, u32[]{:S(2)}, u32[]{:S(2)}) collective-permute-start(bf16[192,512]{1,0:T(8,128)(2,1)} %convolution_convert_fusion.5), channel_id=1, source_target_pairs={{2,0},{3,1},{4,2},{5,3},{6,4},{7,5},{8,6},{9,7},{10,8},{11,9},{12,... | collective-permute-start | bytes 589832 | tf_op jit(solution)/shard_map/ppermute | solution.py:15
  48.2 25.3 %collective-permute-start.9 = (bf16[192,512]{1,0:T(8,128)(2,1)}, bf16[192,512]{1,0:T(8,128)(2,1)}, u32[]{:S(2)}, u32[]{:S(2)}) collective-permute-start(bf16[192,512]{1,0:T(8,128)(2,1)} %convolution_convert_fusion.5), channel_id=1, source_target_pairs={{0,3},{1,4},{2,5},{3,6},{4,7},{5,8},{6,9},{7,10},{8,11},{9,12},{10... | collective-permute-start | bytes 589832 | tf_op jit(solution)/shard_map/ppermute | solution.py:15
  57.1 12.1 %collective-permute-start.8 = (bf16[192,512]{1,0:T(8,128)(2,1)}, bf16[192,512]{1,0:T(8,128)(2,1)}, u32[]{:S(2)}, u32[]{:S(2)}) collective-permute-start(bf16[192,512]{1,0:T(8,128)(2,1)} %convolution_convert_fusion.5), channel_id=1, source_target_pairs={{0,4},{1,5},{2,6},{3,7},{4,8},{5,9},{6,10},{7,11},{8,12},{9,13},{1... | collective-permute-start | bytes 589832 | tf_op jit(solution)/shard_map/ppermute | solution.py:15
  69.1 7.8 %collective-permute-start.10 = (bf16[192,512]{1,0:T(8,128)(2,1)}, bf16[192,512]{1,0:T(8,128)(2,1)S(1)}, u32[]{:S(2)}, u32[]{:S(2)}) collective-permute-start(bf16[192,512]{1,0:T(8,128)(2,1)} %convolution_convert_fusion.5), channel_id=1, source_target_pairs={{0,2},{1,3},{2,4},{3,5},{4,6},{5,7},{6,8},{7,9},{8,10},{9,11},{10,... | collective-permute-start | bytes 589832 | tf_op jit(solution)/shard_map/ppermute | solution.py:15
  73.5 7.3 collective-permute-start.11
  76.9 9.2 %collective-permute-start.12 = (bf16[192,512]{1,0:T(8,128)(2,1)}, bf16[192,512]{1,0:T(8,128)(2,1)S(1)}, u32[]{:S(2)}, u32[]{:S(2)}) collective-permute-start(bf16[192,512]{1,0:T(8,128)(2,1)} %convolution_convert_fusion.5), channel_id=1, source_target_pairs={{1,0},{2,1},{3,2},{4,3},{5,4},{6,5},{7,6},{8,7},{9,8},{10,9},{11,1... | collective-permute-start | bytes 589832 | tf_op jit(solution)/shard_map/ppermute | solution.py:15
  89.0 10.3 %copy-start.3 = (bf16[1728,512]{1,0:T(8,128)(2,1)}, bf16[1728,512]{1,0:T(8,128)(2,1)S(1)}, u32[]{:S(2)}) copy-start(bf16[1728,512]{1,0:T(8,128)(2,1)S(1)} %constant_dynamic-update-slice_fusion) | copy-start | bytes 5308420
  90.9 0.9 copy-start.5
  94.1 1.5 copy-start.1
  100.6 1.5 copy-start.2
  102.3 29.3 %copy-start.4 = (bf16[1,192,1024]{2,1,0:T(8,128)(2,1)S(1)}, bf16[1,192,1024]{2,1,0:T(8,128)(2,1)}, u32[]{:S(2)}) copy-start(bf16[1,192,1024]{2,1,0:T(8,128)(2,1)} %param.6) | copy-start | bytes 1179652
  102.5 15.4 %collective-permute-start.23 = (bf16[192,512]{1,0:T(8,128)(2,1)S(1)}, bf16[192,512]{1,0:T(8,128)(2,1)S(1)}, u32[]{:S(2)}, u32[]{:S(2)}) collective-permute-start(bf16[192,512]{1,0:T(8,128)(2,1)S(1)} %get-tuple-element.13), channel_id=1, source_target_pairs={{0,4},{1,5},{2,6},{3,7},{4,8},{5,9},{6,10},{7,11},{8,12},{9,13},{1... | collective-permute-start | bytes 589832 | tf_op jit(solution)/shard_map/ppermute | solution.py:15
  106.2 12.9 %collective-permute-start.22 = (bf16[192,512]{1,0:T(8,128)(2,1)S(1)}, bf16[192,512]{1,0:T(8,128)(2,1)S(1)}, u32[]{:S(2)}, u32[]{:S(2)}) collective-permute-start(bf16[192,512]{1,0:T(8,128)(2,1)S(1)} %get-tuple-element.14), channel_id=1, source_target_pairs={{4,0},{5,1},{6,2},{7,3},{8,4},{9,5},{10,6},{11,7},{12,8},{13,9},{1... | collective-permute-start | bytes 589832 | tf_op jit(solution)/shard_map/ppermute | solution.py:15
  107.5 16.8 %collective-permute-start.21 = (bf16[192,512]{1,0:T(8,128)(2,1)S(1)}, bf16[192,512]{1,0:T(8,128)(2,1)S(1)}, u32[]{:S(2)}, u32[]{:S(2)}) collective-permute-start(bf16[192,512]{1,0:T(8,128)(2,1)S(1)} %get-tuple-element.15), channel_id=1, source_target_pairs={{0,3},{1,4},{2,5},{3,6},{4,7},{5,8},{6,9},{7,10},{8,11},{9,12},{10... | collective-permute-start | bytes 589832 | tf_op jit(solution)/shard_map/ppermute | solution.py:15
  112.6 13.7 %collective-permute-start.20 = (bf16[192,512]{1,0:T(8,128)(2,1)S(1)}, bf16[192,512]{1,0:T(8,128)(2,1)S(1)}, u32[]{:S(2)}, u32[]{:S(2)}) collective-permute-start(bf16[192,512]{1,0:T(8,128)(2,1)S(1)} %get-tuple-element.16), channel_id=1, source_target_pairs={{3,0},{4,1},{5,2},{6,3},{7,4},{8,5},{9,6},{10,7},{11,8},{12,9},{13... | collective-permute-start | bytes 589832 | tf_op jit(solution)/shard_map/ppermute | solution.py:15
  114.1 12.5 %collective-permute-start.19 = (bf16[192,512]{1,0:T(8,128)(2,1)S(1)}, bf16[192,512]{1,0:T(8,128)(2,1)S(1)}, u32[]{:S(2)}, u32[]{:S(2)}) collective-permute-start(bf16[192,512]{1,0:T(8,128)(2,1)S(1)} %get-tuple-element.17), channel_id=1, source_target_pairs={{0,2},{1,3},{2,4},{3,5},{4,6},{5,7},{6,8},{7,9},{8,10},{9,11},{10,... | collective-permute-start | bytes 589832 | tf_op jit(solution)/shard_map/ppermute | solution.py:15
  117.8 10.2 %collective-permute-start.18 = (bf16[192,512]{1,0:T(8,128)(2,1)S(1)}, bf16[192,512]{1,0:T(8,128)(2,1)S(1)}, u32[]{:S(2)}, u32[]{:S(2)}) collective-permute-start(bf16[192,512]{1,0:T(8,128)(2,1)S(1)} %get-tuple-element.18), channel_id=1, source_target_pairs={{2,0},{3,1},{4,2},{5,3},{6,4},{7,5},{8,6},{9,7},{10,8},{11,9},{12,... | collective-permute-start | bytes 589832 | tf_op jit(solution)/shard_map/ppermute | solution.py:15
  119.1 9.6 %collective-permute-start.17 = (bf16[192,512]{1,0:T(8,128)(2,1)S(1)}, bf16[192,512]{1,0:T(8,128)(2,1)S(1)}, u32[]{:S(2)}, u32[]{:S(2)}) collective-permute-start(bf16[192,512]{1,0:T(8,128)(2,1)S(1)} %get-tuple-element.19), channel_id=1, source_target_pairs={{0,1},{1,2},{2,3},{3,4},{4,5},{5,6},{6,7},{7,8},{8,9},{9,10},{10,1... | collective-permute-start | bytes 589832 | tf_op jit(solution)/shard_map/ppermute | solution.py:15
  124.4 7.0 collective-permute-start.16
Sparse Core Ops, SparseCore 0:
  134.1 587.4 reduce-scatter.3
where the time goes:
time: 759 us; the launch traced here: 751 us
  waiting for transfers between devices  589 us (78%)
  starting transfers between devices  82.6 us (11%)
  blocking collectives  20.9 us (3%)
  local copies, waits for them, and re-layouts  20.3 us (3%)
  matrix products  19.4 us (3%)
  between operations  14.7 us (2%)
    unnamed x2, waiting for transfers between devices  580 us
    ppermute x24, starting transfers between devices, shifted(): lax.ppermute(value, axis, [(source, source + steps) for source in range(l...  82.5 us
    psum x1, blocking collectives, on_device(): grad_weight = lax.psum(share, 'dp')  20.9 us
  transfers between devices with their start and end apart: 25, of which 6 were waited for; matrix products, arithmetic and copies ran while one was open for 3% of the time, Pallas kernels for 0%

commit v1 on v0

--- a/solution.py
+++ b/solution.py
@@ -1,7 +1,13 @@
+import functools
+
 import jax
 import jax.numpy as jnp
 from jax import lax
+from jax.experimental import pallas as pl
+from jax.experimental.pallas import tpu as pltpu
 from jax.sharding import PartitionSpec as P
+
+MESH = pl.DeviceIdType.MESH
 
 HEADS = 8
 KV_HEADS = 2
@@ -65,7 +71,132 @@
     return shifted(parcel, ("outer", "inner"), offset).astype(jnp.float32)
 
 
-def on_device(queries, inputs, kv_weight, grad_out, segment_ids):
+def weight_kernel(
+    n_dp, n_outer, n_inner, in_ref, gkv_ref, out_ref,
+    part, pair_out, pair_in, row_out, row_in, col_out, col_in, dp_buf,
+    pair_send, pair_recv, row_send, row_recv, col_send, col_recv, dp_send, dp_recv,
+):
+    f32, bf16 = jnp.float32, jnp.bfloat16
+    n_x = n_inner // 2
+    dp = lax.axis_index("dp")
+    outer = lax.axis_index("outer")
+    inner = lax.axis_index("inner")
+    x, core = inner // 2, inner % 2
+    sibling = (dp, outer, x * 2 + 1 - core)
+    row_peers = [(dp, outer, lax.rem(x + s, n_x) * 2 + core) for s in range(1, n_x)]
+    col_peers = [(dp, lax.rem(outer + s, n_outer), inner) for s in range(1, n_outer)]
+    dp_peers = [(lax.rem(dp + s, n_dp), outer, inner) for s in range(1, n_dp)]
+    peers = [sibling] + row_peers + col_peers + dp_peers
+
+    barrier = pltpu.get_barrier_semaphore()
+    for peer in peers:
+        pl.semaphore_signal(barrier, inc=1, device_id=peer, device_id_type=MESH)
+
+    grad_kv = gkv_ref[...]
+
+    def product(i, carry):
+        rows = in_ref[:, pl.ds(pl.multiple_of(i * 128, 128), 128)]
+        block = lax.dot_general(rows, grad_kv, (((0,), (0,)), ((), ())), preferred_element_type=f32)
+        for j in range(16):
+            g, at_x, at_core = j // (2 * n_x), (j // 2) % n_x, j % 2
+            piece = block[8 * j : 8 * j + 8, :]
+            piece = jnp.concatenate([piece[:, :256], piece[:, 256:]], axis=0)
+            start = pl.multiple_of((i * 2 + g) * 16, 16)
+            part[at_core, at_x, pl.ds(start, 16), :] = piece
+        return carry
+
+    lax.fori_loop(0, in_ref.shape[1] // 128, product, 0)
+    pair_out[...] = part[1 - core].astype(bf16)
+    pl.semaphore_wait(barrier, len(peers))
+    pair = pltpu.make_async_remote_copy(
+        src_ref=pair_out, dst_ref=pair_in, send_sem=pair_send, recv_sem=pair_recv,
+        device_id=sibling, device_id_type=MESH,
+    )
+    pair.start()
+    pair.wait()
+
+    copies = []
+    for s in range(1, n_x):
+        to = lax.rem(x + s, n_x)
+        row_out[s - 1] = (part[core, to] + pair_in[to].astype(f32)).astype(bf16)
+        copy = pltpu.make_async_remote_copy(
+            src_ref=row_out.at[s - 1], dst_ref=row_in.at[s - 1],
+            send_sem=row_send.at[s - 1], recv_sem=row_recv.at[s - 1],
+            device_id=row_peers[s - 1], device_id_type=MESH,
+        )
+        copy.start()
+        copies.append(copy)
+    total = part[core, x] + pair_in[x].astype(f32)
+    for s, copy in enumerate(copies):
+        copy.wait()
+        total = total + row_in[s].astype(f32)
+    part[core, x] = total
+    col_out[...] = total.astype(bf16)
+
+    copies = []
+    for s in range(1, n_outer):
+        to = lax.rem(outer + s, n_outer)
+        copy = pltpu.make_async_remote_copy(
+            src_ref=col_out.at[pl.ds(pl.multiple_of(to * 16, 16), 16)], dst_ref=col_in.at[s - 1],
+            send_sem=col_send.at[s - 1], recv_sem=col_recv.at[s - 1],
+            device_id=col_peers[s - 1], device_id_type=MESH,
+        )
+        copy.start()
+        copies.append(copy)
+    mine = part[core, x, pl.ds(pl.multiple_of(outer * 16, 16), 16), :]
+    for s, copy in enumerate(copies):
+        copy.wait()
+        mine = mine + col_in[s].astype(f32)
+    dp_buf[dp] = mine
+
+    copies = []
+    for s in range(1, n_dp):
+        copy = pltpu.make_async_remote_copy(
+            src_ref=dp_buf.at[dp], dst_ref=dp_buf.at[dp],
+            send_sem=dp_send.at[s - 1], recv_sem=dp_recv.at[s - 1],
+            device_id=dp_peers[s - 1], device_id_type=MESH,
+        )
+        copy.start()
+        copies.append(copy)
+    for copy in copies:
+        copy.wait()
+    whole = dp_buf[0]
+    for r in range(1, n_dp):
+        whole = whole + dp_buf[r]
+    out_ref[:, :256] = whole[:8]
+    out_ref[:, 256:] = whole[8:]
+
+
+def weight_gradient(mesh, input_rows, grad_kv):
+    f32, bf16 = jnp.float32, jnp.bfloat16
+    n_dp, n_outer, n_inner = mesh.shape["dp"], mesh.shape["outer"], mesh.shape["inner"]
+    n_x = n_inner // 2
+    rows = 16 * n_outer
+    dma = pltpu.SemaphoreType.DMA
+    return pl.pallas_call(
+        functools.partial(weight_kernel, n_dp, n_outer, n_inner),
+        out_shape=jax.ShapeDtypeStruct((8, 512), f32),
+        in_specs=[pl.BlockSpec(memory_space=pltpu.VMEM)] * 2,
+        out_specs=pl.BlockSpec(memory_space=pltpu.VMEM),
+        scratch_shapes=[
+            pltpu.VMEM((2, n_x, rows, 256), f32),
+            pltpu.VMEM((n_x, rows, 256), bf16),
+            pltpu.VMEM((n_x, rows, 256), bf16),
+            pltpu.VMEM((n_x - 1, rows, 256), bf16),
+            pltpu.VMEM((n_x - 1, rows, 256), bf16),
+            pltpu.VMEM((rows, 256), bf16),
+            pltpu.VMEM((n_outer - 1, 16, 256), bf16),
+            pltpu.VMEM((n_dp, 16, 256), f32),
+            dma, dma, dma((n_x - 1,)), dma((n_x - 1,)),
+            dma((n_outer - 1,)), dma((n_outer - 1,)), dma((n_dp - 1,)), dma((n_dp - 1,)),
+        ],
+        compiler_params=pltpu.CompilerParams(
+            collective_id=0, has_side_effects=True, vmem_limit_bytes=32 * 2**20
+        ),
+    )(input_rows, grad_kv)
+
+
+def on_device(mesh, queries, inputs, kv_weight, grad_out, segment_ids):
     query_rows = queries[0]
     input_rows = inputs[0]
     upstream = grad_out[0]
@@ -91,10 +222,7 @@
         total = total + return_direct(parcels[REACH + offset], offset)
     grad_kv = total.astype(jnp.bfloat16)
     grad_input = contract(grad_kv, kv_weight, 1, 1).astype(jnp.bfloat16)
-    share = lax.psum_scatter(
-        contract(input_rows, grad_kv, 0, 0), ("outer", "inner"), scatter_dimension=0, tiled=True
-    )
-    grad_weight = lax.psum(share, "dp")
+    grad_weight = weight_gradient(mesh, input_rows, grad_kv)
     return (grad_query.astype(jnp.bfloat16)[None], grad_input[None], grad_weight)
 
 
@@ -112,5 +240,5 @@
         P(("outer", "inner"), None),
     )
     return jax.shard_map(
-        on_device, mesh=mesh, in_specs=in_specs, out_specs=out_specs, check_vma=False
-    )
+        functools.partial(on_device, mesh), mesh=mesh, in_specs=in_specs, out_specs=out_specs, check_vma=False
+    )

time: 759 us -> 182 us (0.24)
  waiting for transfers between devices: 589 us -> 7.51 us
  Pallas kernels: 0 us -> 51.5 us
  blocking collectives: 20.9 us -> 0 us
  between operations: 14.7 us -> 1.24 us
    unnamed x2 -> x0, waiting for transfers between devices: 580 us -> none
    pallas_call x0 -> x1, Pallas kernels: none -> 51.5 us  [weight_gradient(): pl.pallas_call(functools.partial(weight_kernel, n_dp, n_outer, n_inner),...]
    psum x1 -> x0, blocking collectives: 20.9 us -> none  [on_device(): grad_weight = lax.psum(share, 'dp')]
  transfers between devices with their start and end apart: 25 -> 24, of which waited for: 6 -> 2; matrix products, arithmetic and copies ran while one was open for 3% -> 11% of each run, Pallas kernels for 0% -> 0%
where the time goes in v1:
time: 182 us; the launch traced here: 180 us
  starting transfers between devices  82.6 us (45%)
  Pallas kernels  51.5 us (28%)
  local copies, waits for them, and re-layouts  16.2 us (9%)
  matrix products  15.3 us (8%)
  waiting for transfers between devices  7.51 us (4%)
  other arithmetic  5.23 us (3%)
    ppermute x24, starting transfers between devices, shifted(): lax.ppermute(value, axis, [(source, source + steps) for source in range(l...  82.6 us
    pallas_call x1, Pallas kernels, weight_gradient(): pl.pallas_call(functools.partial(weight_kernel, n_dp, n_outer, n_inner),...  51.5 us
    dot_general x9, matrix products, contract(): lax.dot_general(left, right, (((left_dim,), (right_dim,)), ((), ())), pre...  9.35 us
    ppermute x24, waiting for transfers between devices, shifted(): lax.ppermute(value, axis, [(source, source + steps) for source in range(l...  7.51 us
    reshape x2, local copies, waits for them, and re-layouts, attend(): allowed = jnp.repeat(allowed, per_group, axis=0)  5.58 us
    unnamed x21, local copies, waits for them, and re-layouts  5.44 us
  transfers between devices with their start and end apart: 24, of which 2 were waited for; matrix products, arithmetic and copies ran while one was open for 11% of the time, Pallas kernels for 0%

profile of v1, /device:TPU:1, one launch (start us, length us, event | category | flops | bytes accessed | tf_op | source)
XLA Modules:
  0.0 179.6 jit_solution(17212650735216933983)
XLA Ops:
  1.4 1.3 collective-permute-start.7
  2.7 1.3 collective-permute-start.6
  4.0 1.3 collective-permute-start.5
  5.3 8.8 %collective-permute-start.4 = (s32[192]{0:T(256)S(1)}, s32[192]{0:T(256)S(1)}, u32[]{:S(2)}, u32[]{:S(2)}) collective-permute-start(s32[192]{0:T(256)S(1)} %bitcast.45), channel_id=1, source_target_pairs={{1,0},{2,1},{3,2},{4,3},{5,4},{6,5},{7,6},{8,7},{9,8},{10,9},{11,1... | collective-permute-start | bytes 2312 | tf_op jit(solution)/shard_map/ppermute | solution.py:21
  14.1 4.2 %collective-permute-start.3 = (s32[192]{0:T(256)S(1)}, s32[192]{0:T(256)S(1)}, u32[]{:S(2)}, u32[]{:S(2)}) collective-permute-start(s32[192]{0:T(256)S(1)} %bitcast.46), channel_id=1, source_target_pairs={{0,1},{1,2},{2,3},{3,4},{4,5},{5,6},{6,7},{7,8},{8,9},{9,10},{10,1... | collective-permute-start | bytes 2312 | tf_op jit(solution)/shard_map/ppermute | solution.py:21
  19.4 2.0 %convolution_convert_fusion.5 = bf16[192,512]{1,0:T(8,128)(2,1)} fusion(bf16[1024,512]{1,0:T(8,128)(2,1)S(1)} %copy-done, bf16[1,192,1024]{2,1,0:T(8,128)(2,1)} %param.6), kind=kOutput, calls=%fused_computation.23 | convolution fusion | flops 201424896 | bytes 1638400 | tf_op jit(solution)/shard_map/dot_general | solution.py:205
  21.6 4.3 %collective-permute-start.2 = (s32[192]{0:T(256)S(1)}, s32[192]{0:T(256)S(1)}, u32[]{:S(2)}, u32[]{:S(2)}) collective-permute-start(s32[192]{0:T(256)S(1)} %bitcast.47), channel_id=1, source_target_pairs={{0,2},{1,3},{2,4},{3,5},{4,6},{5,7},{6,8},{7,9},{8,10},{9,11},{10,... | collective-permute-start | bytes 2312 | tf_op jit(solution)/shard_map/ppermute | solution.py:21
  26.0 4.7 %collective-permute-start.1 = (s32[192]{0:T(256)S(1)}, s32[192]{0:T(256)S(1)}, u32[]{:S(2)}, u32[]{:S(2)}) collective-permute-start(s32[192]{0:T(256)S(1)} %bitcast.48), channel_id=1, source_target_pairs={{0,3},{1,4},{2,5},{3,6},{4,7},{5,8},{6,9},{7,10},{8,11},{9,12},{10... | collective-permute-start | bytes 2312 | tf_op jit(solution)/shard_map/ppermute | solution.py:21
  30.7 5.6 %collective-permute-start = (s32[192]{0:T(256)S(1)}, s32[192]{0:T(256)S(1)}, u32[]{:S(2)}, u32[]{:S(2)}) collective-permute-start(s32[192]{0:T(256)S(1)} %bitcast.49), channel_id=1, source_target_pairs={{0,4},{1,5},{2,6},{3,7},{4,8},{5,9},{6,10},{7,11},{8,12},{9,13},{1... | collective-permute-start | bytes 2312 | tf_op jit(solution)/shard_map/ppermute | solution.py:21
  37.7 1.3 collective-permute-start.15
  39.0 1.3 collective-permute-start.14
  40.3 1.3 collective-permute-start.13
  41.6 8.9 %collective-permute-start.9 = (bf16[192,512]{1,0:T(8,128)(2,1)}, bf16[192,512]{1,0:T(8,128)(2,1)}, u32[]{:S(2)}, u32[]{:S(2)}) collective-permute-start(bf16[192,512]{1,0:T(8,128)(2,1)} %convolution_convert_fusion.5), channel_id=1, source_target_pairs={{0,3},{1,4},{2,5},{3,6},{4,7},{5,8},{6,9},{7,10},{8,11},{9,12},{10... | collective-permute-start | bytes 589832 | tf_op jit(solution)/shard_map/ppermute | solution.py:21
  50.5 4.9 %collective-permute-start.8 = (bf16[192,512]{1,0:T(8,128)(2,1)}, bf16[192,512]{1,0:T(8,128)(2,1)}, u32[]{:S(2)}, u32[]{:S(2)}) collective-permute-start(bf16[192,512]{1,0:T(8,128)(2,1)} %convolution_convert_fusion.5), channel_id=1, source_target_pairs={{0,4},{1,5},{2,6},{3,7},{4,8},{5,9},{6,10},{7,11},{8,12},{9,13},{1... | collective-permute-start | bytes 589832 | tf_op jit(solution)/shard_map/ppermute | solution.py:21
  57.0 2.8 %reshape.84 = pred[768,1728]{1,0:T(32,128)(4,1)} reshape(pred[192,4,1728]{2,1,0:T(4,128)(4,1)S(1)} %broadcast_in_dim.9) | data formatting | bytes 2654208 | tf_op jit(solution)/shard_map/reshape | solution.py:35
  59.8 2.8 %copy.8 = pred[768,1728]{0,1:T(32,128)(4,1)S(1)} copy(pred[768,1728]{1,0:T(32,128)(4,1)} %reshape.84) | data formatting | bytes 2654208 | tf_op jit(solution)/shard_map/reshape | solution.py:35
  62.6 3.4 %collective-permute-start.10 = (bf16[192,512]{1,0:T(8,128)(2,1)}, bf16[192,512]{1,0:T(8,128)(2,1)S(1)}, u32[]{:S(2)}, u32[]{:S(2)}) collective-permute-start(bf16[192,512]{1,0:T(8,128)(2,1)} %convolution_convert_fusion.5), channel_id=1, source_target_pairs={{0,2},{1,3},{2,4},{3,5},{4,6},{5,7},{6,8},{7,9},{8,10},{9,11},{10,... | collective-permute-start | bytes 589832 | tf_op jit(solution)/shard_map/ppermute | solution.py:21
  66.9 2.4 %collective-permute-start.11 = (bf16[192,512]{1,0:T(8,128)(2,1)}, bf16[192,512]{1,0:T(8,128)(2,1)S(1)}, u32[]{:S(2)}, u32[]{:S(2)}) collective-permute-start(bf16[192,512]{1,0:T(8,128)(2,1)} %convolution_convert_fusion.5), channel_id=1, source_target_pairs={{0,1},{1,2},{2,3},{3,4},{4,5},{5,6},{6,7},{7,8},{8,9},{9,10},{10,1... | collective-permute-start | bytes 589832 | tf_op jit(solution)/shard_map/ppermute | solution.py:21
  70.3 3.9 %collective-permute-start.12 = (bf16[192,512]{1,0:T(8,128)(2,1)}, bf16[192,512]{1,0:T(8,128)(2,1)S(1)}, u32[]{:S(2)}, u32[]{:S(2)}) collective-permute-start(bf16[192,512]{1,0:T(8,128)(2,1)} %convolution_convert_fusion.5), channel_id=1, source_target_pairs={{1,0},{2,1},{3,2},{4,3},{5,4},{6,5},{7,6},{8,7},{9,8},{10,9},{11,1... | collective-permute-start | bytes 589832 | tf_op jit(solution)/shard_map/ppermute | solution.py:21
  75.2 4.3 %collective-permute-done.12 = bf16[192,512]{1,0:T(8,128)(2,1)S(1)} collective-permute-done((bf16[192,512]{1,0:T(8,128)(2,1)}, bf16[192,512]{1,0:T(8,128)(2,1)S(1)}, u32[]{:S(2)}, u32[]{:S(2)}) %collective-permute-start.12) | collective-permute-done | bytes 196640 | tf_op jit(solution)/shard_map/ppermute | solution.py:21
  94.6 3.8 %collective-permute-start.23 = (bf16[192,512]{1,0:T(8,128)(2,1)S(1)}, bf16[192,512]{1,0:T(8,128)(2,1)S(1)}, u32[]{:S(2)}, u32[]{:S(2)}) collective-permute-start(bf16[192,512]{1,0:T(8,128)(2,1)S(1)} %get-tuple-element.4), channel_id=1, source_target_pairs={{0,4},{1,5},{2,6},{3,7},{4,8},{5,9},{6,10},{7,11},{8,12},{9,13},{1... | collective-permute-start | bytes 589832 | tf_op jit(solution)/shard_map/ppermute | solution.py:21
  98.4 1.3 collective-permute-start.22
  99.7 5.0 %collective-permute-start.21 = (bf16[192,512]{1,0:T(8,128)(2,1)S(1)}, bf16[192,512]{1,0:T(8,128)(2,1)S(1)}, u32[]{:S(2)}, u32[]{:S(2)}) collective-permute-start(bf16[192,512]{1,0:T(8,128)(2,1)S(1)} %get-tuple-element.6), channel_id=1, source_target_pairs={{0,3},{1,4},{2,5},{3,6},{4,7},{5,8},{6,9},{7,10},{8,11},{9,12},{10... | collective-permute-start | bytes 589832 | tf_op jit(solution)/shard_map/ppermute | solution.py:21
  104.7 1.3 collective-permute-start.20
  106.0 4.6 %collective-permute-start.19 = (bf16[192,512]{1,0:T(8,128)(2,1)S(1)}, bf16[192,512]{1,0:T(8,128)(2,1)}, u32[]{:S(2)}, u32[]{:S(2)}) collective-permute-start(bf16[192,512]{1,0:T(8,128)(2,1)S(1)} %get-tuple-element.8), channel_id=1, source_target_pairs={{0,2},{1,3},{2,4},{3,5},{4,6},{5,7},{6,8},{7,9},{8,10},{9,11},{10,... | collective-permute-start | bytes 589832 | tf_op jit(solution)/shard_map/ppermute | solution.py:21
  111.5 1.3 collective-permute-start.18
  112.8 4.6 %collective-permute-start.17 = (bf16[192,512]{1,0:T(8,128)(2,1)S(1)}, bf16[192,512]{1,0:T(8,128)(2,1)}, u32[]{:S(2)}, u32[]{:S(2)}) collective-permute-start(bf16[192,512]{1,0:T(8,128)(2,1)S(1)} %get-tuple-element.10), channel_id=1, source_target_pairs={{0,1},{1,2},{2,3},{3,4},{4,5},{5,6},{6,7},{7,8},{8,9},{9,10},{10,1... | collective-permute-start | bytes 589832 | tf_op jit(solution)/shard_map/ppermute | solution.py:21
  117.4 1.9 %collective-permute-start.16 = (bf16[192,512]{1,0:T(8,128)(2,1)S(1)}, bf16[192,512]{1,0:T(8,128)(2,1)}, u32[]{:S(2)}, u32[]{:S(2)}) collective-permute-start(bf16[192,512]{1,0:T(8,128)(2,1)S(1)} %get-tuple-element.11), channel_id=1, source_target_pairs={{1,0},{2,1},{3,2},{4,3},{5,4},{6,5},{7,6},{8,7},{9,8},{10,9},{11,1... | collective-permute-start | bytes 589832 | tf_op jit(solution)/shard_map/ppermute | solution.py:21
  121.4 3.1 %collective-permute-done.16 = bf16[192,512]{1,0:T(8,128)(2,1)} collective-permute-done((bf16[192,512]{1,0:T(8,128)(2,1)S(1)}, bf16[192,512]{1,0:T(8,128)(2,1)}, u32[]{:S(2)}, u32[]{:S(2)}) %collective-permute-start.16) | collective-permute-done | bytes 196640 | tf_op jit(solution)/shard_map/ppermute | solution.py:21
  124.5 1.6 add_convert_fusion.gkv_ref
  126.2 1.3 fusion.6
  127.4 51.5 %shard_map.76 = f32[8,512]{1,0:T(8,128)S(1)} custom-call(bf16[192,1024]{1,0:T(8,128)(2,1)S(1)} %bitcast.39, bf16[192,512]{1,0:T(8,128)(2,1)S(1)} %add_convert_fusion.gkv_ref), custom_call_target="tpu_custom_call" | custom-call | tf_op jit(solution)/shard_map/pallas_call | solution.py:176
  (77 shorter events, 26.3 us)
Async XLA Ops:
  0.6 18.7 %copy-start = (bf16[1024,512]{1,0:T(8,128)(2,1)S(1)}, bf16[1024,512]{1,0:T(8,128)(2,1)}, u32[]{:S(2)}) copy-start(bf16[1024,512]{1,0:T(8,128)(2,1)} %param.7) | copy-start | bytes 3145732
  0.6 20.8 %copy-start.3 = (bf16[1,192,1024]{2,1,0:T(8,128)(2,1)S(1)}, bf16[1,192,1024]{2,1,0:T(8,128)(2,1)}, u32[]{:S(2)}) copy-start(bf16[1,192,1024]{2,1,0:T(8,128)(2,1)} %param.8) | copy-start | bytes 1179652
  1.4 20.1 %collective-permute-start.7 = (s32[192]{0:T(256)S(1)}, s32[192]{0:T(256)S(1)}, u32[]{:S(2)}, u32[]{:S(2)}) collective-permute-start(s32[192]{0:T(256)S(1)} %bitcast.42), channel_id=1, source_target_pairs={{4,0},{5,1},{6,2},{7,3},{8,4},{9,5},{10,6},{11,7},{12,8},{13,9},{1... | collective-permute-start | bytes 2312 | tf_op jit(solution)/shard_map/ppermute | solution.py:21
  2.7 23.2 %collective-permute-start.6 = (s32[192]{0:T(256)S(1)}, s32[192]{0:T(256)S(1)}, u32[]{:S(2)}, u32[]{:S(2)}) collective-permute-start(s32[192]{0:T(256)S(1)} %bitcast.43), channel_id=1, source_target_pairs={{3,0},{4,1},{5,2},{6,3},{7,4},{8,5},{9,6},{10,7},{11,8},{12,9},{13... | collective-permute-start | bytes 2312 | tf_op jit(solution)/shard_map/ppermute | solution.py:21
  4.0 26.7 %collective-permute-start.5 = (s32[192]{0:T(256)S(1)}, s32[192]{0:T(256)S(1)}, u32[]{:S(2)}, u32[]{:S(2)}) collective-permute-start(s32[192]{0:T(256)S(1)} %bitcast.44), channel_id=1, source_target_pairs={{2,0},{3,1},{4,2},{5,3},{6,4},{7,5},{8,6},{9,7},{10,8},{11,9},{12,... | collective-permute-start | bytes 2312 | tf_op jit(solution)/shard_map/ppermute | solution.py:21
  5.3 32.3 %collective-permute-start.4 = (s32[192]{0:T(256)S(1)}, s32[192]{0:T(256)S(1)}, u32[]{:S(2)}, u32[]{:S(2)}) collective-permute-start(s32[192]{0:T(256)S(1)} %bitcast.45), channel_id=1, source_target_pairs={{1,0},{2,1},{3,2},{4,3},{5,4},{6,5},{7,6},{8,7},{9,8},{10,9},{11,1... | collective-permute-start | bytes 2312 | tf_op jit(solution)/shard_map/ppermute | solution.py:21
  14.1 24.8 %collective-permute-start.3 = (s32[192]{0:T(256)S(1)}, s32[192]{0:T(256)S(1)}, u32[]{:S(2)}, u32[]{:S(2)}) collective-permute-start(s32[192]{0:T(256)S(1)} %bitcast.46), channel_id=1, source_target_pairs={{0,1},{1,2},{2,3},{3,4},{4,5},{5,6},{6,7},{7,8},{8,9},{9,10},{10,1... | collective-permute-start | bytes 2312 | tf_op jit(solution)/shard_map/ppermute | solution.py:21
  21.6 18.7 %collective-permute-start.2 = (s32[192]{0:T(256)S(1)}, s32[192]{0:T(256)S(1)}, u32[]{:S(2)}, u32[]{:S(2)}) collective-permute-start(s32[192]{0:T(256)S(1)} %bitcast.47), channel_id=1, source_target_pairs={{0,2},{1,3},{2,4},{3,5},{4,6},{5,7},{6,8},{7,9},{8,10},{9,11},{10,... | collective-permute-start | bytes 2312 | tf_op jit(solution)/shard_map/ppermute | solution.py:21
  26.0 15.6 %collective-permute-start.1 = (s32[192]{0:T(256)S(1)}, s32[192]{0:T(256)S(1)}, u32[]{:S(2)}, u32[]{:S(2)}) collective-permute-start(s32[192]{0:T(256)S(1)} %bitcast.48), channel_id=1, source_target_pairs={{0,3},{1,4},{2,5},{3,6},{4,7},{5,8},{6,9},{7,10},{8,11},{9,12},{10... | collective-permute-start | bytes 2312 | tf_op jit(solution)/shard_map/ppermute | solution.py:21
  30.7 19.8 %collective-permute-start = (s32[192]{0:T(256)S(1)}, s32[192]{0:T(256)S(1)}, u32[]{:S(2)}, u32[]{:S(2)}) collective-permute-start(s32[192]{0:T(256)S(1)} %bitcast.49), channel_id=1, source_target_pairs={{0,4},{1,5},{2,6},{3,7},{4,8},{5,9},{6,10},{7,11},{8,12},{9,13},{1... | collective-permute-start | bytes 2312 | tf_op jit(solution)/shard_map/ppermute | solution.py:21
  37.7 43.8 %collective-permute-start.15 = (bf16[192,512]{1,0:T(8,128)(2,1)}, bf16[192,512]{1,0:T(8,128)(2,1)}, u32[]{:S(2)}, u32[]{:S(2)}) collective-permute-start(bf16[192,512]{1,0:T(8,128)(2,1)} %convolution_convert_fusion.5), channel_id=1, source_target_pairs={{4,0},{5,1},{6,2},{7,3},{8,4},{9,5},{10,6},{11,7},{12,8},{13,9},{1... | collective-permute-start | bytes 589832 | tf_op jit(solution)/shard_map/ppermute | solution.py:21
  39.0 41.6 %collective-permute-start.14 = (bf16[192,512]{1,0:T(8,128)(2,1)}, bf16[192,512]{1,0:T(8,128)(2,1)}, u32[]{:S(2)}, u32[]{:S(2)}) collective-permute-start(bf16[192,512]{1,0:T(8,128)(2,1)} %convolution_convert_fusion.5), channel_id=1, source_target_pairs={{3,0},{4,1},{5,2},{6,3},{7,4},{8,5},{9,6},{10,7},{11,8},{12,9},{13... | collective-permute-start | bytes 589832 | tf_op jit(solution)/shard_map/ppermute | solution.py:21
  40.3 39.3 %collective-permute-start.13 = (bf16[192,512]{1,0:T(8,128)(2,1)}, bf16[192,512]{1,0:T(8,128)(2,1)}, u32[]{:S(2)}, u32[]{:S(2)}) collective-permute-start(bf16[192,512]{1,0:T(8,128)(2,1)} %convolution_convert_fusion.5), channel_id=1, source_target_pairs={{2,0},{3,1},{4,2},{5,3},{6,4},{7,5},{8,6},{9,7},{10,8},{11,9},{12,... | collective-permute-start | bytes 589832 | tf_op jit(solution)/shard_map/ppermute | solution.py:21
  41.6 25.3 %collective-permute-start.9 = (bf16[192,512]{1,0:T(8,128)(2,1)}, bf16[192,512]{1,0:T(8,128)(2,1)}, u32[]{:S(2)}, u32[]{:S(2)}) collective-permute-start(bf16[192,512]{1,0:T(8,128)(2,1)} %convolution_convert_fusion.5), channel_id=1, source_target_pairs={{0,3},{1,4},{2,5},{3,6},{4,7},{5,8},{6,9},{7,10},{8,11},{9,12},{10... | collective-permute-start | bytes 589832 | tf_op jit(solution)/shard_map/ppermute | solution.py:21
  50.5 12.1 %collective-permute-start.8 = (bf16[192,512]{1,0:T(8,128)(2,1)}, bf16[192,512]{1,0:T(8,128)(2,1)}, u32[]{:S(2)}, u32[]{:S(2)}) collective-permute-start(bf16[192,512]{1,0:T(8,128)(2,1)} %convolution_convert_fusion.5), channel_id=1, source_target_pairs={{0,4},{1,5},{2,6},{3,7},{4,8},{5,9},{6,10},{7,11},{8,12},{9,13},{1... | collective-permute-start | bytes 589832 | tf_op jit(solution)/shard_map/ppermute | solution.py:21
  62.6 7.8 %collective-permute-start.10 = (bf16[192,512]{1,0:T(8,128)(2,1)}, bf16[192,512]{1,0:T(8,128)(2,1)S(1)}, u32[]{:S(2)}, u32[]{:S(2)}) collective-permute-start(bf16[192,512]{1,0:T(8,128)(2,1)} %convolution_convert_fusion.5), channel_id=1, source_target_pairs={{0,2},{1,3},{2,4},{3,5},{4,6},{5,7},{6,8},{7,9},{8,10},{9,11},{10,... | collective-permute-start | bytes 589832 | tf_op jit(solution)/shard_map/ppermute | solution.py:21
  66.9 7.3 %collective-permute-start.11 = (bf16[192,512]{1,0:T(8,128)(2,1)}, bf16[192,512]{1,0:T(8,128)(2,1)S(1)}, u32[]{:S(2)}, u32[]{:S(2)}) collective-permute-start(bf16[192,512]{1,0:T(8,128)(2,1)} %convolution_convert_fusion.5), channel_id=1, source_target_pairs={{0,1},{1,2},{2,3},{3,4},{4,5},{5,6},{6,7},{7,8},{8,9},{9,10},{10,1... | collective-permute-start | bytes 589832 | tf_op jit(solution)/shard_map/ppermute | solution.py:21
  70.3 9.2 %collective-permute-start.12 = (bf16[192,512]{1,0:T(8,128)(2,1)}, bf16[192,512]{1,0:T(8,128)(2,1)S(1)}, u32[]{:S(2)}, u32[]{:S(2)}) collective-permute-start(bf16[192,512]{1,0:T(8,128)(2,1)} %convolution_convert_fusion.5), channel_id=1, source_target_pairs={{1,0},{2,1},{3,2},{4,3},{5,4},{6,5},{7,6},{8,7},{9,8},{10,9},{11,1... | collective-permute-start | bytes 589832 | tf_op jit(solution)/shard_map/ppermute | solution.py:21
  84.3 0.9 copy-start.2
  94.6 17.0 %collective-permute-start.23 = (bf16[192,512]{1,0:T(8,128)(2,1)S(1)}, bf16[192,512]{1,0:T(8,128)(2,1)S(1)}, u32[]{:S(2)}, u32[]{:S(2)}) collective-permute-start(bf16[192,512]{1,0:T(8,128)(2,1)S(1)} %get-tuple-element.4), channel_id=1, source_target_pairs={{0,4},{1,5},{2,6},{3,7},{4,8},{5,9},{6,10},{7,11},{8,12},{9,13},{1... | collective-permute-start | bytes 589832 | tf_op jit(solution)/shard_map/ppermute | solution.py:21
  98.4 14.5 %collective-permute-start.22 = (bf16[192,512]{1,0:T(8,128)(2,1)S(1)}, bf16[192,512]{1,0:T(8,128)(2,1)S(1)}, u32[]{:S(2)}, u32[]{:S(2)}) collective-permute-start(bf16[192,512]{1,0:T(8,128)(2,1)S(1)} %get-tuple-element.5), channel_id=1, source_target_pairs={{4,0},{5,1},{6,2},{7,3},{8,4},{9,5},{10,6},{11,7},{12,8},{13,9},{1... | collective-permute-start | bytes 589832 | tf_op jit(solution)/shard_map/ppermute | solution.py:21
  99.7 17.8 %collective-permute-start.21 = (bf16[192,512]{1,0:T(8,128)(2,1)S(1)}, bf16[192,512]{1,0:T(8,128)(2,1)S(1)}, u32[]{:S(2)}, u32[]{:S(2)}) collective-permute-start(bf16[192,512]{1,0:T(8,128)(2,1)S(1)} %get-tuple-element.6), channel_id=1, source_target_pairs={{0,3},{1,4},{2,5},{3,6},{4,7},{5,8},{6,9},{7,10},{8,11},{9,12},{10... | collective-permute-start | bytes 589832 | tf_op jit(solution)/shard_map/ppermute | solution.py:21
  104.7 16.7 %collective-permute-start.20 = (bf16[192,512]{1,0:T(8,128)(2,1)S(1)}, bf16[192,512]{1,0:T(8,128)(2,1)}, u32[]{:S(2)}, u32[]{:S(2)}) collective-permute-start(bf16[192,512]{1,0:T(8,128)(2,1)S(1)} %get-tuple-element.7), channel_id=1, source_target_pairs={{3,0},{4,1},{5,2},{6,3},{7,4},{8,5},{9,6},{10,7},{11,8},{12,9},{13... | collective-permute-start | bytes 589832 | tf_op jit(solution)/shard_map/ppermute | solution.py:21
  106.0 15.4 %collective-permute-start.19 = (bf16[192,512]{1,0:T(8,128)(2,1)S(1)}, bf16[192,512]{1,0:T(8,128)(2,1)}, u32[]{:S(2)}, u32[]{:S(2)}) collective-permute-start(bf16[192,512]{1,0:T(8,128)(2,1)S(1)} %get-tuple-element.8), channel_id=1, source_target_pairs={{0,2},{1,3},{2,4},{3,5},{4,6},{5,7},{6,8},{7,9},{8,10},{9,11},{10,... | collective-permute-start | bytes 589832 | tf_op jit(solution)/shard_map/ppermute | solution.py:21
  111.5 9.9 %collective-permute-start.18 = (bf16[192,512]{1,0:T(8,128)(2,1)S(1)}, bf16[192,512]{1,0:T(8,128)(2,1)}, u32[]{:S(2)}, u32[]{:S(2)}) collective-permute-start(bf16[192,512]{1,0:T(8,128)(2,1)S(1)} %get-tuple-element.9), channel_id=1, source_target_pairs={{2,0},{3,1},{4,2},{5,3},{6,4},{7,5},{8,6},{9,7},{10,8},{11,9},{12,... | collective-permute-start | bytes 589832 | tf_op jit(solution)/shard_map/ppermute | solution.py:21
  112.8 6.5 %copy-start.4 = (bf16[192,512]{1,0:T(8,128)(2,1)}, bf16[192,512]{1,0:T(8,128)(2,1)S(1)}, u32[]{:S(2)}) copy-start(bf16[192,512]{1,0:T(8,128)(2,1)S(1)} %collective-permute-done.22) | copy-start | bytes 589828
  112.8 8.6 %collective-permute-start.17 = (bf16[192,512]{1,0:T(8,128)(2,1)S(1)}, bf16[192,512]{1,0:T(8,128)(2,1)}, u32[]{:S(2)}, u32[]{:S(2)}) collective-permute-start(bf16[192,512]{1,0:T(8,128)(2,1)S(1)} %get-tuple-element.10), channel_id=1, source_target_pairs={{0,1},{1,2},{2,3},{3,4},{4,5},{5,6},{6,7},{7,8},{8,9},{9,10},{10,1... | collective-permute-start | bytes 589832 | tf_op jit(solution)/shard_map/ppermute | solution.py:21
  117.4 2.0 %copy-start.5 = (bf16[192,512]{1,0:T(8,128)(2,1)}, bf16[192,512]{1,0:T(8,128)(2,1)S(1)}, u32[]{:S(2)}) copy-start(bf16[192,512]{1,0:T(8,128)(2,1)S(1)} %collective-permute-done.21) | copy-start | bytes 589828
  117.4 7.1 %collective-permute-start.16 = (bf16[192,512]{1,0:T(8,128)(2,1)S(1)}, bf16[192,512]{1,0:T(8,128)(2,1)}, u32[]{:S(2)}, u32[]{:S(2)}) collective-permute-start(bf16[192,512]{1,0:T(8,128)(2,1)S(1)} %get-tuple-element.11), channel_id=1, source_target_pairs={{1,0},{2,1},{3,2},{4,3},{5,4},{6,5},{7,6},{8,7},{9,8},{10,9},{11,1... | collective-permute-start | bytes 589832 | tf_op jit(solution)/shard_map/ppermute | solution.py:21
  120.3 7.1 %copy-start.1 = (bf16[1,192,1024]{2,1,0:T(8,128)(2,1)S(1)}, bf16[1,192,1024]{2,1,0:T(8,128)(2,1)}, u32[]{:S(2)}) copy-start(bf16[1,192,1024]{2,1,0:T(8,128)(2,1)} %param.6) | copy-start | bytes 1179652

commit v2 on v1

v2 whole, which is shorter than its diff:
```python
import functools
import math

import jax
import jax.numpy as jnp
from jax import lax
from jax.experimental import pallas as pl
from jax.experimental.pallas import tpu as pltpu
from jax.sharding import PartitionSpec as P

MESH = pl.DeviceIdType.MESH
HEADS = 8
GROUPS = 2
PER_GROUP = HEADS // GROUPS
HEAD = 128
TOK = 192
PAIR = 2 * TOK
SENT = TOK + 16
WIDTH = 2 * GROUPS * HEAD
MODEL = HEADS * HEAD
SPAN = 5
HERE = 2
FACTOR = HEAD**-0.5
LOG2E = math.log2(math.e)
FAR = -1e30
F32 = jnp.float32
BF16 = jnp.bfloat16


def product(left, right, left_dim, right_dim):
    return lax.dot_general(
        left, right, (((left_dim,), (right_dim,)), ((), ())), preferred_element_type=F32
    )


def thrice(rows):
    return jnp.concatenate([rows, rows, rows], axis=1)


def columns(index):
    return pl.ds(pl.multiple_of(index * HEAD, HEAD), HEAD)


def remote(source, target, send, recv, device):
    return pltpu.make_async_remote_copy(
        src_ref=source, dst_ref=target, send_sem=send, recv_sem=recv,
        device_id=device, device_id_type=MESH,
    )


def kernel(
    n_dp, n_outer, n_inner,
    q_hbm, in_hbm, w_hbm, up_hbm, ids_ref,
    dq_hbm, dx_hbm, gw_ref,
    raw, rows_in, weight, queries, upstream,
    window, ids_col, scores, grads, peak, total, dots,
    probs_low, grad_scores, grad_query,
    own, sib_out, sib_in, ring_out, ring_in, grad_kv,
    dq_out, dx_out,
    part, pair_out, pair_in, row_out, row_in, col_out, col_in, dp_buf,
    load_sem, store_sem,
    halo_send, halo_recv, sib_send, sib_recv, ring_send, ring_recv,
    pair_send, pair_recv, row_send, row_recv, col_send, col_recv, dp_send, dp_recv,
):
    n_x = n_inner // 2
    chips = n_outer * n_x
    dp = lax.axis_index("dp")
    outer = lax.axis_index("outer")
    inner = lax.axis_index("inner")
    x, core = inner // 2, inner % 2
    chip = outer * n_x + x

    def chip_at(steps):
        there = lax.rem(chip + steps + chips, chips)
        return (dp, there // n_x, lax.rem(there, n_x) * 2 + core)

    sibling = (dp, outer, x * 2 + 1 - core)
    right, left = chip_at(1), chip_at(-1)
    row_peers = [(dp, outer, lax.rem(x + s, n_x) * 2 + core) for s in range(1, n_x)]
    col_peers = [(dp, lax.rem(outer + s, n_outer), inner) for s in range(1, n_outer)]
    dp_peers = [(lax.rem(dp + s, n_dp), outer, inner) for s in range(1, n_dp)]
    peers = [sibling, right, left] + row_peers + col_peers + dp_peers

    barrier = pltpu.get_barrier_semaphore()
    for peer in peers:
        pl.semaphore_signal(barrier, inc=1, device_id=peer, device_id_type=MESH)

    loads = [
        pltpu.make_async_copy(source, target, load_sem.at[i])
        for i, (source, target) in enumerate(
            [(in_hbm, rows_in), (w_hbm, weight), (q_hbm, raw.at[0]), (up_hbm, raw.at[1])]
        )
    ]
    for load in loads:
        load.start()

    ids_row = ids_ref[...].astype(F32)
    twice = jnp.concatenate([ids_row, ids_row, jnp.zeros((1, WIDTH - PAIR), F32)], axis=1)
    window[HERE, 0, TOK:SENT, :] = jnp.broadcast_to(twice, (SENT - TOK, WIDTH)).astype(BF16)
    ids_col[...] = jnp.transpose(jnp.broadcast_to(twice[:, :256], (HEAD, 256)))[:TOK]

    loads[0].wait()
    loads[1].wait()
    window[HERE, 0, 0:TOK, :] = product(rows_in[...], weight[...], 1, 0).astype(BF16)
    pl.semaphore_wait(barrier, len(peers))

    halo = [
        remote(source, target, halo_send.at[i], halo_recv.at[i], device)
        for i, (source, target, device) in enumerate(
            [
                (window.at[2, 0], window.at[2, 1], sibling),
                (window.at[2, 0], window.at[1, 0], right),
                (window.at[2, 0], window.at[3, 0], left),
                (window.at[1, 0], window.at[0, 0], right),
                (window.at[3, 0], window.at[4, 0], left),
                (window.at[1, 0], window.at[1, 1], sibling),
                (window.at[3, 0], window.at[3, 1], sibling),
                (window.at[0, 0], window.at[0, 1], sibling),
                (window.at[4, 0], window.at[4, 1], sibling),
            ]
        )
    ]
    for i in (1, 2, 0):
        halo[i].start()

    loads[2].wait()
    loads[3].wait()
    for h in range(HEADS):
        at = slice(h * HEAD, (h + 1) * HEAD)
        queries[h] = raw[0, :, at]
        upstream[h] = raw[1, :, at]

    def keys_of(j, at):
        return jnp.concatenate(
            [window[j, 0, 0:TOK, columns(at)], window[j, 1, 0:TOK, columns(at)]], axis=0
        )

    def first_pass(j, opening):
        lane = lax.broadcasted_iota(jnp.int32, (1, PAIR), 1)
        ids_key = jnp.where(
            lane < TOK,
            window[j, 0, TOK:SENT, :PAIR].astype(F32)[:1],
            window[j, 1, TOK:SENT, :PAIR].astype(F32)[:1],
        )
        mask = jnp.where(thrice(ids_col[...]) == ids_key, 0.0, FAR)

        def group(g, carry):
            keys = keys_of(j, g)
            values = keys_of(j, GROUPS + g)
            for member in range(PER_GROUP):
                h = g * PER_GROUP + member
                score = product(queries[h], keys, 1, 1) * (FACTOR * LOG2E) + mask
                grad = product(upstream[h], values, 1, 1)
                scores[j, h] = score
                grads[j, h] = grad
                top = jnp.maximum(
                    jnp.maximum(score[:, :128], score[:, 128:256]), score[:, 256:]
                )
                if not opening:
                    before = peak[h]
                    top = jnp.maximum(before, top)
                weights = jnp.exp2(score - thrice(top))
                dot = weights * grad
                weights = weights[:, :128] + weights[:, 128:256] + weights[:, 256:]
                dot = dot[:, :128] + dot[:, 128:256] + dot[:, 256:]
                if not opening:
                    scale = jnp.exp2(before - top)
                    weights = weights + total[h] * scale
                    dot = dot + dots[h] * scale
                peak[h] = top
                total[h] = weights
                dots[h] = dot
            return carry

        lax.fori_loop(0, GROUPS, group, 0)

    halo[0].wait_recv()
    first_pass(HERE, True)
    halo[1].wait_recv()
    halo[3].start()
    halo[5].start()
    halo[2].wait_recv()
    halo[4].start()
    halo[6].start()
    halo[5].wait_recv()
    halo[6].wait_recv()

    def near(t, carry):
        first_pass(1 + 2 * t, False)
        return carry

    lax.fori_loop(0, 2, near, 0)
    halo[3].wait_recv()
    halo[7].start()
    halo[4].wait_recv()
    halo[8].start()
    halo[7].wait_recv()
    halo[8].wait_recv()

    def distant(t, carry):
        first_pass(4 * t, False)
        return carry

    lax.fori_loop(0, 2, distant, 0)

    def merge(h, carry):
        top = jnp.max(peak[h], axis=1, keepdims=True)
        scale = jnp.exp2(peak[h] - top)
        weights = jnp.sum(total[h] * scale, axis=1, keepdims=True)
        dot = jnp.sum(dots[h] * scale, axis=1, keepdims=True) / weights
        peak[h] = jnp.broadcast_to(top + jnp.log(weights) * LOG2E, (TOK, HEAD))
        dots[h] = jnp.broadcast_to(dot, (TOK, HEAD))
        return carry

    lax.fori_loop(0, HEADS, merge, 0)

    def second_pass(j, opening):
        def group(g, carry):
            for member in range(PER_GROUP):
                h = g * PER_GROUP + member
                probs = jnp.exp2(scores[j, h] - thrice(peak[h]))
                at = slice(member * TOK, (member + 1) * TOK)
                probs_low[at, :] = probs.astype(BF16)
                grad_scores[at, :] = (probs * (grads[j, h] - thrice(dots[h]))).astype(BF16)
            low = grad_scores[...]
            part_query = product(low, keys_of(j, g), 1, 0)
            start = g * PER_GROUP
            query = queries[pl.ds(start, PER_GROUP)].reshape(PER_GROUP * TOK, HEAD)
            up = upstream[pl.ds(start, PER_GROUP)].reshape(PER_GROUP * TOK, HEAD)
            if opening:
                grad_query[g] = part_query
            else:
                grad_query[g] = grad_query[g] + part_query
            key = product(low, query, 0, 0) * FACTOR
            value = product(probs_low[...], up, 0, 0)
            own[j, :, columns(g)] = key[:TOK]
            own[j, :, columns(GROUPS + g)] = value[:TOK]
            sib_out[j, :, columns(g)] = key[TOK:].astype(BF16)
            sib_out[j, :, columns(GROUPS + g)] = value[TOK:].astype(BF16)
            return carry

        lax.fori_loop(0, GROUPS, group, 0)

    sib = [
        remote(sib_out.at[j], sib_in.at[j], sib_send.at[j], sib_recv.at[j], sibling)
        for j in range(SPAN)
    ]
    ring = [
        remote(ring_out.at[i], ring_in.at[i], ring_send.at[i], ring_recv.at[i], device)
        for i, device in enumerate([left, right, left, right])
    ]

    second_pass(0, True)
    sib[0].start()
    second_pass(4, False)
    sib[4].start()
    for i, j in enumerate((0, 4)):
        sib[j].wait_recv()
        ring_out[i] = (own[j] + sib_in[j].astype(F32)).astype(BF16)
        ring[i].start()
    second_pass(1, False)
    sib[1].start()
    second_pass(3, False)
    sib[3].start()
    for i, j in enumerate((1, 3)):
        sib[j].wait_recv()
        ring[i].wait_recv()
        ring_out[2 + i] = (
            own[j] + sib_in[j].astype(F32) + ring_in[i].astype(F32)
        ).astype(BF16)
        ring[2 + i].start()
    second_pass(2, False)
    sib[2].start()
    for h in range(HEADS):
        at = slice((h % PER_GROUP) * TOK, (h % PER_GROUP + 1) * TOK)
        dq_out[:, h * HEAD : (h + 1) * HEAD] = (
            grad_query[h // PER_GROUP, at, :] * FACTOR
        ).astype(BF16)
    dq_store = pltpu.make_async_copy(dq_out, dq_hbm, store_sem.at[0])
    dq_store.start()
    sib[2].wait_recv()
    ring[2].wait_recv()
    ring[3].wait_recv()
    grad_kv[...] = (
        own[2] + sib_in[2].astype(F32) + ring_in[2].astype(F32) + ring_in[3].astype(F32)
    ).astype(BF16)

    def weight_rows(i, carry):
        block = product(rows_in[:, pl.ds(pl.multiple_of(i * 128, 128), 128)], grad_kv[...], 0, 0)
        for j in range(16):
            g, at_x, at_core = j // (2 * n_x), (j // 2) % n_x, j % 2
            piece = block[8 * j : 8 * j + 8, :]
            piece = jnp.concatenate([piece[:, :256], piece[:, 256:]], axis=0)
            start = pl.multiple_of((i * 2 + g) * 16, 16)
            part[at_core, at_x, pl.ds(start, 16), :] = piece
        return carry

    lax.fori_loop(0, MODEL // 128, weight_rows, 0)
    pair_out[...] = part[1 - core].astype(BF16)
    pair = remote(pair_out, pair_in, pair_send, pair_recv, sibling)
    pair.start()
    dx_out[...] = product(grad_kv[...], weight[...], 1, 1).astype(BF16)
    dx_store = pltpu.make_async_copy(dx_out, dx_hbm, store_sem.at[1])
    dx_store.start()
    pair.wait()

    copies = []
    for s in range(1, n_x):
        to = lax.rem(x + s, n_x)
        row_out[s - 1] = (part[core, to] + pair_in[to].astype(F32)).astype(BF16)
        copy = remote(
            row_out.at[s - 1], row_in.at[s - 1], row_send.at[s - 1], row_recv.at[s - 1],
            row_peers[s - 1],
        )
        copy.start()
        copies.append(copy)
    mine = part[core, x] + pair_in[x].astype(F32)
    for s, copy in enumerate(copies):
        copy.wait()
        mine = mine + row_in[s].astype(F32)
    part[core, x] = mine
    col_out[...] = mine.astype(BF16)

    copies = []
    for s in range(1, n_outer):
        to = lax.rem(outer + s, n_outer)
        copy = remote(
            col_out.at[pl.ds(pl.multiple_of(to * 16, 16), 16)], col_in.at[s - 1],
            col_send.at[s - 1], col_recv.at[s - 1], col_peers[s - 1],
        )
        copy.start()
        copies.append(copy)
    mine = part[core, x, pl.ds(pl.multiple_of(outer * 16, 16), 16), :]
    for s, copy in enumerate(copies):
        copy.wait()
        mine = mine + col_in[s].astype(F32)
    dp_buf[dp] = mine

    copies = []
    for s in range(1, n_dp):
        copy = remote(
            dp_buf.at[dp], dp_buf.at[dp], dp_send.at[s - 1], dp_recv.at[s - 1], dp_peers[s - 1]
        )
        copy.start()
        copies.append(copy)
    for copy in copies:
        copy.wait()
    whole = dp_buf[0]
    for r in range(1, n_dp):
        whole = whole + dp_buf[r]
    gw_ref[:, :256] = whole[:8]
    gw_ref[:, 256:] = whole[8:]

    for copy in halo + sib + ring:
        copy.wait_send()
    dq_store.wait()
    dx_store.wait()


def on_device(sizes, queries, inputs, kv_weight, grad_out, segment_ids):
    n_dp, n_outer, n_inner = sizes
    n_x = n_inner // 2
    rows = 16 * n_outer
    vmem, dma = pltpu.VMEM, pltpu.SemaphoreType.DMA
    anywhere = pl.BlockSpec(memory_space=pl.ANY)
    inside = pl.BlockSpec(memory_space=pltpu.VMEM)
    tokens = jax.ShapeDtypeStruct((TOK, MODEL), BF16)
    grad_query, grad_input, grad_weight = pl.pallas_call(
        functools.partial(kernel, *sizes),
        out_shape=(tokens, tokens, jax.ShapeDtypeStruct((8, WIDTH), F32)),
        in_specs=[anywhere] * 4 + [inside],
        out_specs=(anywhere, anywhere, inside),
        scratch_shapes=[
            vmem((2, TOK, MODEL), BF16),
            vmem((TOK, MODEL), BF16),
            vmem((MODEL, WIDTH), BF16),
            vmem((HEADS, TOK, HEAD), BF16),
            vmem((HEADS, TOK, HEAD), BF16),
            vmem((SPAN, 2, SENT, WIDTH), BF16),
            vmem((TOK, HEAD), F32),
            vmem((SPAN, HEADS, TOK, PAIR), F32),
            vmem((SPAN, HEADS, TOK, PAIR), F32),
            vmem((HEADS, TOK, HEAD), F32),
            vmem((HEADS, TOK, HEAD), F32),
            vmem((HEADS, TOK, HEAD), F32),
            vmem((PER_GROUP * TOK, PAIR), BF16),
            vmem((PER_GROUP * TOK, PAIR), BF16),
            vmem((GROUPS, PER_GROUP * TOK, HEAD), F32),
            vmem((SPAN, TOK, WIDTH), F32),
            vmem((SPAN, TOK, WIDTH), BF16),
            vmem((SPAN, TOK, WIDTH), BF16),
            vmem((4, TOK, WIDTH), BF16),
            vmem((4, TOK, WIDTH), BF16),
            vmem((TOK, WIDTH), BF16),
            vmem((TOK, MODEL), BF16),
            vmem((TOK, MODEL), BF16),
            vmem((2, n_x, rows, 256), F32),
            vmem((n_x, rows, 256), BF16),
            vmem((n_x, rows, 256), BF16),
            vmem((n_x - 1, rows, 256), BF16),
            vmem((n_x - 1, rows, 256), BF16),
            vmem((rows, 256), BF16),
            vmem((n_outer - 1, 16, 256), BF16),
            vmem((n_dp, 16, 256), F32),
            dma((4,)), dma((2,)),
            dma((9,)), dma((9,)), dma((SPAN,)), dma((SPAN,)), dma((4,)), dma((4,)),
            dma, dma, dma((n_x - 1,)), dma((n_x - 1,)),
            dma((n_outer - 1,)), dma((n_outer - 1,)), dma((n_dp - 1,)), dma((n_dp - 1,)),
        ],
        compiler_params=pltpu.CompilerParams(
            collective_id=0, has_side_effects=True, vmem_limit_bytes=56 * 2**20
        ),
    )(queries[0], inputs[0], kv_weight, grad_out[0], segment_ids)
    return grad_query[None], grad_input[None], grad_weight


def solution(mesh):
    spread = P("dp", ("outer", "inner"), None)
    sizes = (mesh.shape["dp"], mesh.shape["outer"], mesh.shape["inner"])
    return jax.shard_map(
        functools.partial(on_device, sizes),
        mesh=mesh,
        in_specs=(spread, spread, P(), spread, P("dp", ("outer", "inner"))),
        out_specs=(spread, spread, P(("outer", "inner"), None)),
        check_vma=False,
    )
```

time: 182 us -> 78.9 us (0.43)
  the two profiles are of different devices: /device:TPU:1 before, /device:TPU:4 now
where the time goes in v2:
time: 78.9 us; the launch traced here: 78.7 us
  Pallas kernels  74.9 us (95%)
  local copies, waits for them, and re-layouts  3.18 us (4%)
    pallas_call x1, Pallas kernels, on_device(): pl.pallas_call(functools.partial(kernel, *sizes), out_shape=(tokens, toke...  74.9 us
    unnamed x7, local copies, waits for them, and re-layouts  3.18 us

profile of v2, /device:TPU:4, one launch (start us, length us, event | category | flops | bytes accessed | tf_op | source)
XLA Modules:
  0.0 78.7 jit_solution(4676704972624175362)
XLA Ops:
  0.6 74.9 %shard_map.76 = (bf16[192,1024]{1,0:T(8,128)(2,1)}, bf16[192,1024]{1,0:T(8,128)(2,1)}, f32[8,512]{1,0:T(8,128)}) custom-call(bf16[192,1024]{1,0:T(8,128)(2,1)} %bitcast.7, bf16[192,1024]{1,0:T(8,128)(2,1)} %bitcast.8, bf16[1024,512]{1,0:T(8,128)(2,1)} %w_hbm.1, bf16[192,1024]{1,0:T(8,128)(2,1)} %bitcast.9, s32[1,192]{1,0:T(1,128)} %ids_ref.1), custom_call_target="tpu_custom_call" | custom-call | tf_op jit(solution)/shard_map/pallas_call | solution.py:368
  75.5 0.0 copy-start
  75.5 1.8 %copy.11 = bf16[1,192,1024]{2,1,0:T(8,128)(2,1)} copy(bf16[1,192,1024]{2,1,0:T(8,128)(2,1)} %bitcast.6) | data formatting | bytes 786432
  77.4 0.0 copy-done
  77.4 0.0 copy-start.1
  77.4 0.7 copy.12
  78.1 0.0 copy-done.1
  78.1 0.6 copy.13
Async XLA Ops:
  75.5 1.8 %copy-start = (bf16[192,1024]{1,0:T(8,128)(2,1)S(1)}, bf16[192,1024]{1,0:T(8,128)(2,1)}, u32[]{:S(2)}) copy-start(bf16[192,1024]{1,0:T(8,128)(2,1)} %get-tuple-element.7) | copy-start | bytes 1179652
  77.4 0.8 copy-start.1

commit v3 on v0

v3 whole, which is shorter than its diff:
```python
import functools
import math

import jax
import jax.numpy as jnp
from jax import lax
from jax.experimental import pallas as pl
from jax.experimental.pallas import tpu as pltpu
from jax.sharding import PartitionSpec as P

MESH = pl.DeviceIdType.MESH
HEADS = 8
GROUPS = 2
PER_GROUP = HEADS // GROUPS
HEAD = 128
TOK = 192
PAIR = 2 * TOK
SENT = TOK + 16
HALF = 2 * HEAD
TILES = PAIR // 8
WIDTH = 2 * GROUPS * HEAD
MODEL = HEADS * HEAD
SPAN = 5
HERE = 2
FACTOR = HEAD**-0.5
LOG2E = math.log2(math.e)
FAR = -1e30
F32 = jnp.float32
BF16 = jnp.bfloat16


def product(left, right, left_dim, right_dim):
    return lax.dot_general(
        left, right, (((left_dim,), (right_dim,)), ((), ())), preferred_element_type=F32
    )


def thrice(rows):
    return jnp.concatenate([rows, rows, rows], axis=1)


def remote(source, target, send, recv, device):
    return pltpu.make_async_remote_copy(
        src_ref=source, dst_ref=target, send_sem=send, recv_sem=recv,
        device_id=device, device_id_type=MESH,
    )


def kernel(
    n_dp, n_outer, n_inner,
    q_hbm, in_hbm, w_hbm, up_hbm, ids_ref,
    dq_hbm, dx_hbm, gw_ref,
    raw, rows_in, rows_sib, weight, queries, upstream,
    window, ids_query, mask, scores, grads, peak, total, dots, grad_query,
    own, sib_out, sib_in, ring_out, ring_in, grad_kv, grad_kv_sib,
    dq_out, dx_out,
    part, row_out, row_in, col_out, col_in, mine, dp_buf,
    load_sem, store_sem,
    halo_send, halo_recv, rows_send, rows_recv, sib_send, sib_recv, ring_send, ring_recv,
    pair_send, pair_recv, row_send, row_recv, col_send, col_recv, dp_send, dp_recv,
):
    n_x = n_inner // 2
    chips = n_outer * n_x
    dp = lax.axis_index("dp")
    outer = lax.axis_index("outer")
    inner = lax.axis_index("inner")
    x, core = inner // 2, inner % 2
    chip = outer * n_x + x

    def chip_at(steps):
        there = lax.rem(chip + steps + chips, chips)
        return (dp, there // n_x, lax.rem(there, n_x) * 2 + core)

    sibling = (dp, outer, x * 2 + 1 - core)
    right, left = chip_at(1), chip_at(-1)
    row_right = (dp, outer, lax.rem(x + 1, n_x) * 2 + core)
    row_left = (dp, outer, lax.rem(x + n_x - 1, n_x) * 2 + core)
    col_peers = [(dp, lax.rem(outer + s, n_outer), inner) for s in range(1, n_outer)]
    dp_peers = [
        (s, flip, (lax.rem(dp + s, n_dp), outer, x * 2 + (1 - core if flip else core)))
        for s in range(n_dp)
        for flip in (0, 1)
        if s or flip
    ]
    peers = [right, left, row_right, row_left] + col_peers + [peer for _, _, peer in dp_peers]

    barrier = pltpu.get_barrier_semaphore()
    for peer in peers:
        pl.semaphore_signal(barrier, inc=1, device_id=peer, device_id_type=MESH)

    loads = [
        pltpu.make_async_copy(source, target, load_sem.at[i])
        for i, (source, target) in enumerate(
            [(in_hbm, rows_in), (w_hbm, weight), (q_hbm, raw.at[0]), (up_hbm, raw.at[1])]
        )
    ]
    for load in loads:
        load.start()

    ids_row = ids_ref[...].astype(F32)
    twice = jnp.concatenate([ids_row, ids_row, jnp.zeros((1, 2 * HALF - PAIR), F32)], axis=1)
    first_row = lax.broadcasted_iota(jnp.int32, (SENT - TOK, HALF), 0) == 0
    window[HERE, 0, 0, TOK:SENT, :] = jnp.where(
        first_row, twice[:, :HALF], twice[:, HALF:]
    ).astype(BF16)
    ids_query[...] = jnp.broadcast_to(twice[:, :PAIR], (8, PAIR))

    loads[0].wait()
    loads[1].wait()
    key_value = product(rows_in[...], weight[...], 1, 0).astype(BF16)
    for g in range(GROUPS):
        window[HERE, 0, g, 0:TOK, :HEAD] = key_value[:, g * HEAD : (g + 1) * HEAD]
        window[HERE, 0, g, 0:TOK, HEAD:] = key_value[
            :, (GROUPS + g) * HEAD : (GROUPS + g + 1) * HEAD
        ]
    pl.semaphore_wait(barrier, len(peers))

    halo = []
    for g in range(GROUPS):
        rows = pl.ds(0, TOK if g else SENT)
        for i, (source, target, device) in enumerate(
            [
                ((2, 0), (2, 1), sibling),
                ((2, 0), (1, 0), right),
                ((2, 0), (3, 0), left),
                ((1, 0), (0, 0), right),
                ((3, 0), (4, 0), left),
                ((1, 0), (1, 1), sibling),
                ((3, 0), (3, 1), sibling),
                ((0, 0), (0, 1), sibling),
                ((4, 0), (4, 1), sibling),
            ]
        ):
            halo.append(
                remote(
                    window.at[source[0], source[1], g, rows],
                    window.at[target[0], target[1], g, rows],
                    halo_send.at[9 * g + i], halo_recv.at[9 * g + i], device,
                )
            )
    for g in range(GROUPS):
        for i in (1, 2, 0):
            halo[9 * g + i].start()
    rows_copy = remote(rows_in, rows_sib, rows_send, rows_recv, sibling)
    rows_copy.start()

    loads[2].wait()
    loads[3].wait()
    for h in range(HEADS):
        g, member = h // PER_GROUP, h % PER_GROUP
        at = slice(h * HEAD, (h + 1) * HEAD)
        queries[g, member * TOK : (member + 1) * TOK, :] = raw[0, :, at]
        upstream[g, member * TOK : (member + 1) * TOK, :] = raw[1, :, at]

    def of_chunk(j, g, at):
        return jnp.concatenate([window[j, 0, g, 0:TOK, at], window[j, 1, g, 0:TOK, at]], axis=0)

    keys_at, values_at = slice(0, HEAD), slice(HEAD, HALF)

    def make_mask(j):
        lane = lax.broadcasted_iota(jnp.int32, (1, PAIR), 1)
        near, far = (
            jnp.concatenate([ids[0:1], ids[1:2, : PAIR - HALF]], axis=1)
            for ids in (window[j, side, 0, TOK:SENT, :].astype(F32) for side in (0, 1))
        )
        ids_key = jnp.where(lane < TOK, near, far)
        ids_col = jnp.transpose(jnp.broadcast_to(ids_key, (HEAD, PAIR)))
        mask[j] = jnp.where(thrice(ids_col) == ids_query[0:1, :], 0.0, FAR)

    def first_pass(j, g, opening):
        keys, values = of_chunk(j, g, keys_at), of_chunk(j, g, values_at)
        for b in range(2):
            at = slice(b * PAIR, (b + 1) * PAIR)
            score = product(keys, queries[g, at, :], 1, 1) * (FACTOR * LOG2E) + mask[j]
            grad = product(values, upstream[g, at, :], 1, 1)
            scores[j, g, b] = score
            grads[j, g, b] = grad
            score = score.reshape(TILES, 8, PAIR)
            top = jnp.max(score, axis=0)
            if not opening:
                before = peak[g, b]
                top = jnp.maximum(before, top)
            weights = jnp.exp2(score - top[None])
            dot = jnp.sum(weights * grad.reshape(TILES, 8, PAIR), axis=0)
            weights = jnp.sum(weights, axis=0)
            if not opening:
                scale = jnp.exp2(before - top)
                weights = weights + total[g, b] * scale
                dot = dot + dots[g, b] * scale
            peak[g, b] = top
            total[g, b] = weights
            dots[g, b] = dot

    def both(visit, first, stride):
        def step(t, carry):
            visit(first + stride * t)
            return carry

        lax.fori_loop(0, 2, step, 0)

    def merge(g):
        for b in range(2):
            top = jnp.max(peak[g, b], axis=0, keepdims=True)
            scale = jnp.exp2(peak[g, b] - top)
            weights = jnp.sum(total[g, b] * scale, axis=0, keepdims=True)
            dot = jnp.sum(dots[g, b] * scale, axis=0, keepdims=True) / weights
            peak[g, b] = jnp.broadcast_to(top + jnp.log(weights) * LOG2E, (8, PAIR))
            dots[g, b] = jnp.broadcast_to(dot, (8, PAIR))

    def second_pass(j, g, opening):
        keys = of_chunk(j, g, keys_at)
        key, value = 0.0, 0.0
        for b in range(2):
            at = slice(b * PAIR, (b + 1) * PAIR)
            probs = jnp.exp2(scores[j, g, b].reshape(TILES, 8, PAIR) - peak[g, b][None])
            low = probs.reshape(PAIR, PAIR).astype(BF16)
            grad = probs * (grads[j, g, b].reshape(TILES, 8, PAIR) - dots[g, b][None])
            grad = grad.reshape(PAIR, PAIR).astype(BF16)
            key = key + product(grad, queries[g, at, :], 1, 0)
            value = value + product(low, upstream[g, at, :], 1, 0)
            query = product(keys, grad, 0, 0)
            grad_query[g, b] = query if opening else grad_query[g, b] + query
        key = key * FACTOR
        own[j, g, :, :HEAD] = key[:TOK]
        own[j, g, :, HEAD:] = value[:TOK]
        sib_out[j, g, :, :HEAD] = key[TOK:].astype(BF16)
        sib_out[j, g, :, HEAD:] = value[TOK:].astype(BF16)

    sib = [
        [
            remote(
                sib_out.at[j, g], sib_in.at[j, g],
                sib_send.at[GROUPS * j + g], sib_recv.at[GROUPS * j + g], sibling,
            )
            for g in range(GROUPS)
        ]
        for j in range(SPAN)
    ]
    ring = [
        [
            remote(
                ring_out.at[i, g], ring_in.at[i, g],
                ring_send.at[GROUPS * i + g], ring_recv.at[GROUPS * i + g], device,
            )
            for g in range(GROUPS)
        ]
        for i, device in enumerate([left, right, left, right])
    ]

    def near_arrived(g):
        halo[9 * g + 1].wait_recv()
        halo[9 * g + 3].start()
        halo[9 * g + 2].wait_recv()
        halo[9 * g + 4].start()
        halo[9 * g + 5].start()
        halo[9 * g + 6].start()

    def distant_arrived(g):
        halo[9 * g + 3].wait_recv()
        halo[9 * g + 7].start()
        halo[9 * g + 4].wait_recv()
        halo[9 * g + 8].start()

    def send_distant(g):
        for i, j in enumerate((0, 4)):
            sib[j][g].wait_recv()
            ring_out[i, g] = (own[j, g] + sib_in[j, g].astype(F32)).astype(BF16)
            ring[i][g].start()

    def send_near(g):
        for i, j in enumerate((1, 3)):
            sib[j][g].wait_recv()
            ring[i][g].wait_recv()
            ring_out[2 + i, g] = (
                own[j, g] + sib_in[j, g].astype(F32) + ring_in[i, g].astype(F32)
            ).astype(BF16)
            ring[2 + i][g].start()

    halo[0].wait_recv()
    make_mask(HERE)
    first_pass(HERE, 0, True)
    halo[9].wait_recv()
    first_pass(HERE, 1, True)

    near_arrived(0)
    halo[5].wait_recv()
    halo[6].wait_recv()
    both(make_mask, 1, 2)
    both(lambda j: first_pass(j, 0, False), 1, 2)
    near_arrived(1)
    halo[14].wait_recv()
    halo[15].wait_recv()
    both(lambda j: first_pass(j, 1, False), 1, 2)

    distant_arrived(0)
    halo[7].wait_recv()
    halo[8].wait_recv()
    both(make_mask, 0, 4)
    both(lambda j: first_pass(j, 0, False), 0, 4)
    merge(0)
    grad_query[...] = jnp.zeros_like(grad_query)
    distant_arrived(1)
    both(lambda j: second_pass(j, 0, False), 0, 4)
    sib[0][0].start()
    sib[4][0].start()
    halo[16].wait_recv()
    halo[17].wait_recv()
    both(lambda j: first_pass(j, 1, False), 0, 4)
    send_distant(0)
    merge(1)
    both(lambda j: second_pass(j, 1, False), 0, 4)
    sib[0][1].start()
    sib[4][1].start()
    both(lambda j: second_pass(j, 0, False), 1, 2)
    sib[1][0].start()
    sib[3][0].start()
    send_distant(1)
    send_near(0)
    both(lambda j: second_pass(j, 1, False), 1, 2)
    sib[1][1].start()
    sib[3][1].start()
    second_pass(HERE, 0, False)
    sib[2][0].start()
    send_near(1)
    second_pass(HERE, 1, False)
    sib[2][1].start()

    for g in range(GROUPS):
        for b in range(2):
            rows = jnp.transpose(grad_query[g, b]) * FACTOR
            for m in range(2):
                h = g * PER_GROUP + 2 * b + m
                dq_out[:, h * HEAD : (h + 1) * HEAD] = rows[m * TOK : (m + 1) * TOK].astype(BF16)
    dq_store = pltpu.make_async_copy(dq_out, dq_hbm, store_sem.at[0])
    dq_store.start()

    for g in range(GROUPS):
        sib[2][g].wait_recv()
        ring[2][g].wait_recv()
        ring[3][g].wait_recv()
        grad_kv[g] = (
            own[2, g] + sib_in[2, g].astype(F32)
            + ring_in[2, g].astype(F32) + ring_in[3, g].astype(F32)
        ).astype(BF16)
    pair = remote(grad_kv.at[1 - core], grad_kv_sib, pair_send, pair_recv, sibling)
    pair.start()
    rows_copy.wait_recv()
    pair.wait_recv()

    def weight_rows(i, carry):
        at = pl.ds(pl.multiple_of(i * 128, 128), 128)
        block = product(rows_in[:, at], grad_kv[core], 0, 0)
        block = block + product(rows_sib[:, at], grad_kv_sib[...], 0, 0)
        for s in range(128 // (16 * n_x)):
            start = pl.multiple_of((i * (128 // (16 * n_x)) + s) * 16, 16)
            for to in range(n_x):
                lo = (s * n_x + to) * 16
                part[to, pl.ds(start, 16), :] = block[lo : lo + 16, :]
        return carry

    lax.fori_loop(0, MODEL // 128, weight_rows, 0)

    rows_x = 16 * n_outer // 2
    top, bottom = pl.ds(0, rows_x), pl.ds(rows_x, rows_x)
    at_right, at_left = lax.rem(x + 1, n_x), lax.rem(x + n_x - 1, n_x)
    opposite = lax.rem(x + 2, n_x)
    row = [
        remote(row_out.at[i], row_in.at[i], row_send.at[i], row_recv.at[i], device)
        for i, device in enumerate(
            [row_right, row_left, row_right, row_left, row_right, row_left]
        )
    ]
    for i, (to, rows) in enumerate(
        [(opposite, top), (opposite, bottom), (at_right, bottom), (at_left, top)]
    ):
        row_out[i] = part[to, rows, :].astype(BF16)
        row[i].start()
    kv_rows = jnp.concatenate(
        [grad_kv[0, :, :HEAD], grad_kv[1, :, :HEAD], grad_kv[0, :, HEAD:], grad_kv[1, :, HEAD:]],
        axis=1,
    )
    dx_out[...] = product(kv_rows, weight[...], 1, 1).astype(BF16)
    dx_store = pltpu.make_async_copy(dx_out, dx_hbm, store_sem.at[1])
    dx_store.start()
    for i, (to, rows) in enumerate([(at_right, top), (at_left, bottom)]):
        row[i].wait_recv()
        row_out[4 + i] = (part[to, rows, :] + row_in[i].astype(F32)).astype(BF16)
        row[4 + i].start()
    for i in range(2, 6):
        row[i].wait_recv()
    upper = part[x, top, :] + row_in[3].astype(F32) + row_in[4].astype(F32)
    lower = part[x, bottom, :] + row_in[2].astype(F32) + row_in[5].astype(F32)
    part[x, top, :] = upper
    part[x, bottom, :] = lower
    col_out[top, :] = upper.astype(BF16)
    col_out[bottom, :] = lower.astype(BF16)

    col = []
    for s in range(1, n_outer):
        to = lax.rem(outer + s, n_outer)
        copy = remote(
            col_out.at[pl.ds(pl.multiple_of(to * 16, 16), 16)], col_in.at[s - 1],
            col_send.at[s - 1], col_recv.at[s - 1], col_peers[s - 1],
        )
        copy.start()
        col.append(copy)
    share = part[x, pl.ds(pl.multiple_of(outer * 16, 16), 16), :]
    for s, copy in enumerate(col):
        copy.wait_recv()
        share = share + col_in[s].astype(F32)
    mine[...] = share

    last = []
    for i, (s, flip, peer) in enumerate(dp_peers):
        half = 1 - core if flip else core
        copy = remote(
            mine.at[pl.ds(pl.multiple_of(half * 8, 8), 8)], dp_buf.at[dp, core],
            dp_send.at[i], dp_recv.at[i], peer,
        )
        copy.start()
        last.append(copy)
    dp_buf[dp, core] = mine[pl.ds(pl.multiple_of(core * 8, 8), 8), :]
    for copy in last:
        copy.wait_recv()
    for g in range(GROUPS):
        whole = dp_buf[0, g]
        for r in range(1, n_dp):
            whole = whole + dp_buf[r, g]
        gw_ref[:, g * HEAD : (g + 1) * HEAD] = whole[:, :HEAD]
        gw_ref[:, (GROUPS + g) * HEAD : (GROUPS + g + 1) * HEAD] = whole[:, HEAD:]

    for copy in halo + sum(sib, []) + sum(ring, []) + [rows_copy, pair] + row + col + last:
        copy.wait_send()
    dq_store.wait()
    dx_store.wait()


def on_device(sizes, queries, inputs, kv_weight, grad_out, segment_ids):
    n_dp, n_outer, n_inner = sizes
    n_x = n_inner // 2
    rows = 16 * n_outer
    vmem, dma = pltpu.VMEM, pltpu.SemaphoreType.DMA
    anywhere = pl.BlockSpec(memory_space=pl.ANY)
    inside = pl.BlockSpec(memory_space=pltpu.VMEM)
    tokens = jax.ShapeDtypeStruct((TOK, MODEL), BF16)
    grad_query, grad_input, grad_weight = pl.pallas_call(
        functools.partial(kernel, *sizes),
        out_shape=(tokens, tokens, jax.ShapeDtypeStruct((8, WIDTH), F32)),
        in_specs=[anywhere] * 4 + [inside],
        out_specs=(anywhere, anywhere, inside),
        scratch_shapes=[
            vmem((2, TOK, MODEL), BF16),
            vmem((TOK, MODEL), BF16),
            vmem((TOK, MODEL), BF16),
            vmem((MODEL, WIDTH), BF16),
            vmem((GROUPS, PER_GROUP * TOK, HEAD), BF16),
            vmem((GROUPS, PER_GROUP * TOK, HEAD), BF16),
            vmem((SPAN, 2, GROUPS, SENT, HALF), BF16),
            vmem((8, PAIR), F32),
            vmem((SPAN, PAIR, PAIR), F32),
            vmem((SPAN, GROUPS, 2, PAIR, PAIR), F32),
            vmem((SPAN, GROUPS, 2, PAIR, PAIR), F32),
            vmem((GROUPS, 2, 8, PAIR), F32),
            vmem((GROUPS, 2, 8, PAIR), F32),
            vmem((GROUPS, 2, 8, PAIR), F32),
            vmem((GROUPS, 2, HEAD, PAIR), F32),
            vmem((SPAN, GROUPS, TOK, HALF), F32),
            vmem((SPAN, GROUPS, TOK, HALF), BF16),
            vmem((SPAN, GROUPS, TOK, HALF), BF16),
            vmem((4, GROUPS, TOK, HALF), BF16),
            vmem((4, GROUPS, TOK, HALF), BF16),
            vmem((GROUPS, TOK, HALF), BF16),
            vmem((TOK, HALF), BF16),
            vmem((TOK, MODEL), BF16),
            vmem((TOK, MODEL), BF16),
            vmem((n_x, rows, HALF), F32),
            vmem((6, rows // 2, HALF), BF16),
            vmem((6, rows // 2, HALF), BF16),
            vmem((rows, HALF), BF16),
            vmem((n_outer - 1, 16, HALF), BF16),
            vmem((16, HALF), F32),
            vmem((n_dp, 2, 8, HALF), F32),
            dma((4,)), dma((2,)),
            dma((18,)), dma((18,)), dma, dma, dma((10,)), dma((10,)), dma((8,)), dma((8,)),
            dma, dma, dma((6,)), dma((6,)),
            dma((n_outer - 1,)), dma((n_outer - 1,)), dma((2 * n_dp - 1,)), dma((2 * n_dp - 1,)),
        ],
        compiler_params=pltpu.CompilerParams(
            collective_id=0, has_side_effects=True, vmem_limit_bytes=56 * 2**20
        ),
    )(queries[0], inputs[0], kv_weight, grad_out[0], segment_ids)
    return grad_query[None], grad_input[None], grad_weight


def solution(mesh):
    spread = P("dp", ("outer", "inner"), None)
    sizes = (mesh.shape["dp"], mesh.shape["outer"], mesh.shape["inner"])
    return jax.shard_map(
        functools.partial(on_device, sizes),
        mesh=mesh,
        in_specs=(spread, spread, P(), spread, P("dp", ("outer", "inner"))),
        out_specs=(spread, spread, P(("outer", "inner"), None)),
        check_vma=False,
    )
```

time: 759 us -> 73.2 us (0.10); the launches traced: 751 us -> 73 us
  waiting for transfers between devices: 589 us -> 0 us
  starting transfers between devices: 82.6 us -> 0 us
  Pallas kernels: 0 us -> 69.2 us
  blocking collectives: 20.9 us -> 0 us
  matrix products: 19.4 us -> 0 us
  local copies, waits for them, and re-layouts: 20.3 us -> 3.18 us
  between operations: 14.7 us -> 0.65 us
    unnamed x2 -> x0, waiting for transfers between devices: 580 us -> none
    ppermute x24 -> x0, starting transfers between devices: 82.5 us -> none  [shifted(): lax.ppermute(value, axis, [(source, source + steps) for source in range(l...]
    pallas_call x0 -> x1, Pallas kernels: none -> 69.2 us  [on_device(): pl.pallas_call(functools.partial(kernel, *sizes), out_shape=(tokens, toke...]
    psum x1 -> x0, blocking collectives: 20.9 us -> none  [on_device(): grad_weight = lax.psum(share, 'dp')]
    dot_general x15 -> x0, matrix products: 19.4 us -> none  [the longest x10 9.82 us: contract(): lax.dot_general(left, right, (((left_dim,), (right_dim,)), ((), ())), pre...]
    ppermute x24 -> x0, waiting for transfers between devices: 9.45 us -> none  [shifted(): lax.ppermute(value, axis, [(source, source + steps) for source in range(l...]
  transfers between devices with their start and end apart: 25 -> 0, of which waited for: 6 -> 0; matrix products, arithmetic and copies ran while one was open for 3% -> 0% of each run, Pallas kernels for 0% -> 0%
where the time goes in v3:
time: 73.2 us; the launch traced here: 73 us
  Pallas kernels  69.2 us (95%)
  local copies, waits for them, and re-layouts  3.18 us (4%)
    pallas_call x1, Pallas kernels, on_device(): pl.pallas_call(functools.partial(kernel, *sizes), out_shape=(tokens, toke...  69.2 us
    unnamed x7, local copies, waits for them, and re-layouts  3.18 us

profile of v3, /device:TPU:1, one launch (start us, length us, event | category | flops | bytes accessed | tf_op | source)
XLA Modules:
  0.0 73.0 jit_solution(11359846940070995117)
XLA Ops:
  0.6 69.2 %shard_map.76 = (bf16[192,1024]{1,0:T(8,128)(2,1)}, bf16[192,1024]{1,0:T(8,128)(2,1)}, f32[8,512]{1,0:T(8,128)}) custom-call(bf16[192,1024]{1,0:T(8,128)(2,1)} %bitcast.7, bf16[192,1024]{1,0:T(8,128)(2,1)} %bitcast.8, bf16[1024,512]{1,0:T(8,128)(2,1)} %w_hbm.1, bf16[192,1024]{1,0:T(8,128)(2,1)} %bitcast.9, s32[1,192]{1,0:T(1,128)} %ids_ref.1), custom_call_target="tpu_custom_call" | custom-call | tf_op jit(solution)/shard_map/pallas_call | solution.py:446
  69.8 0.0 copy-start
  69.8 1.8 %copy.11 = bf16[1,192,1024]{2,1,0:T(8,128)(2,1)} copy(bf16[1,192,1024]{2,1,0:T(8,128)(2,1)} %bitcast.6) | data formatting | bytes 786432
  71.6 0.0 copy-done
  71.6 0.0 copy-start.1
  71.6 0.7 %copy.12 = bf16[1,192,1024]{2,1,0:T(8,128)(2,1)} copy(bf16[1,192,1024]{2,1,0:T(8,128)(2,1)S(1)} %bitcast.5) | data formatting | bytes 786432
  72.4 0.0 copy-done.1
  72.4 0.6 copy.13
Async XLA Ops:
  69.8 1.8 %copy-start = (bf16[192,1024]{1,0:T(8,128)(2,1)S(1)}, bf16[192,1024]{1,0:T(8,128)(2,1)}, u32[]{:S(2)}) copy-start(bf16[192,1024]{1,0:T(8,128)(2,1)} %get-tuple-element.7) | copy-start | bytes 1179652
  71.6 0.8 %copy-start.1 = (f32[8,512]{1,0:T(8,128)S(1)}, f32[8,512]{1,0:T(8,128)}, u32[]{:S(2)}) copy-start(f32[8,512]{1,0:T(8,128)} %get-tuple-element.14) | copy-start | bytes 49156

commit v4 on v3

--- a/solution.py
+++ b/solution.py
@@ -49,13 +49,12 @@
 def kernel(
     n_dp, n_outer, n_inner,
     q_hbm, in_hbm, w_hbm, up_hbm, ids_ref,
-    dq_hbm, dx_hbm, gw_ref,
-    raw, rows_in, rows_sib, weight, queries, upstream,
+    dq_out, dx_out, gw_ref,
+    raw, rows_in, rows_sib, rows_turned, weight, queries, upstream,
     window, ids_query, mask, scores, grads, peak, total, dots, grad_query,
     own, sib_out, sib_in, ring_out, ring_in, grad_kv, grad_kv_sib,
-    dq_out, dx_out,
     part, row_out, row_in, col_out, col_in, mine, dp_buf,
-    load_sem, store_sem,
+    load_sem,
     halo_send, halo_recv, rows_send, rows_recv, sib_send, sib_recv, ring_send, ring_recv,
     pair_send, pair_recv, row_send, row_recv, col_send, col_recv, dp_send, dp_recv,
 ):
@@ -73,16 +72,23 @@
 
     sibling = (dp, outer, x * 2 + 1 - core)
     right, left = chip_at(1), chip_at(-1)
-    row_right = (dp, outer, lax.rem(x + 1, n_x) * 2 + core)
-    row_left = (dp, outer, lax.rem(x + n_x - 1, n_x) * 2 + core)
-    col_peers = [(dp, lax.rem(outer + s, n_outer), inner) for s in range(1, n_outer)]
+    row_order = sorted(range(1, n_x), key=lambda s: -min(s, n_x - s))
+    row_peers = [(dp, outer, lax.rem(x + s, n_x) * 2 + core) for s in row_order]
+    n_y = n_outer // 2
+    z, y = outer // n_y, outer % n_y
+    col_order = sorted(
+        ((sz, sy) for sy in range(n_y) for sz in range(2) if sy or sz),
+        key=lambda s: (-min(s[1], n_y - s[1]), -s[0], s[1]),
+    )
+    col_at = [lax.rem(z + sz, 2) * n_y + lax.rem(y + sy, n_y) for sz, sy in col_order]
+    col_peers = [(dp, at, inner) for at in col_at]
     dp_peers = [
         (s, flip, (lax.rem(dp + s, n_dp), outer, x * 2 + (1 - core if flip else core)))
         for s in range(n_dp)
         for flip in (0, 1)
         if s or flip
     ]
-    peers = [right, left, row_right, row_left] + col_peers + [peer for _, _, peer in dp_peers]
+    peers = [right, left] + row_peers + col_peers + [peer for _, _, peer in dp_peers]
 
     barrier = pltpu.get_barrier_semaphore()
     for peer in peers:
@@ -105,7 +111,10 @@
     ).astype(BF16)
     ids_query[...] = jnp.broadcast_to(twice[:, :PAIR], (8, PAIR))
 
+    pl.semaphore_wait(barrier, len(peers))
     loads[0].wait()
+    rows_copy = remote(rows_in, rows_sib, rows_send, rows_recv, sibling)
+    rows_copy.start()
     loads[1].wait()
     key_value = product(rows_in[...], weight[...], 1, 0).astype(BF16)
     for g in range(GROUPS):
@@ -113,8 +122,6 @@
         window[HERE, 0, g, 0:TOK, HEAD:] = key_value[
             :, (GROUPS + g) * HEAD : (GROUPS + g + 1) * HEAD
         ]
-    pl.semaphore_wait(barrier, len(peers))
-
     halo = []
     for g in range(GROUPS):
         rows = pl.ds(0, TOK if g else SENT)
@@ -141,8 +148,6 @@
     for g in range(GROUPS):
         for i in (1, 2, 0):
             halo[9 * g + i].start()
-    rows_copy = remote(rows_in, rows_sib, rows_send, rows_recv, sibling)
-    rows_copy.start()
 
     loads[2].wait()
     loads[3].wait()
@@ -247,6 +252,17 @@
         for i, device in enumerate([left, right, left, right])
     ]
 
+    def turn_inputs():
+        rows_copy.wait_recv()
+
+        def turn(i, carry):
+            at = pl.ds(pl.multiple_of(i * 128, 128), 128)
+            rows = jnp.concatenate([rows_in[:, at], rows_sib[:, at]], axis=0)
+            rows_turned[at, :] = jnp.transpose(rows)
+            return carry
+
+        lax.fori_loop(0, MODEL // 128, turn, 0)
+
     def near_arrived(g):
         halo[9 * g + 1].wait_recv()
         halo[9 * g + 3].start()
@@ -282,6 +298,7 @@
     halo[9].wait_recv()
     first_pass(HERE, 1, True)
 
+    turn_inputs()
     near_arrived(0)
     halo[5].wait_recv()
     halo[6].wait_recv()
@@ -325,133 +342,152 @@
     second_pass(HERE, 1, False)
     sib[2][1].start()
 
+    pair = [
+        remote(
+            grad_kv.at[g, 1 - core], grad_kv_sib.at[g], pair_send.at[g], pair_recv.at[g], sibling
+        )
+        for g in range(GROUPS)
+    ]
+    row = [
+        [
+            remote(
+                row_out.at[g, i], row_in.at[g, i],
+                row_send.at[(n_x - 1) * g + i], row_recv.at[(n_x - 1) * g + i], row_peers[i],
+            )
+            for i in range(n_x - 1)
+        ]
+        for g in range(GROUPS)
+    ]
+    col = [
+        [
+            remote(
+                col_out.at[g, col_at[i]], col_in.at[g, i],
+                col_send.at[(n_outer - 1) * g + i], col_recv.at[(n_outer - 1) * g + i],
+                col_peers[i],
+            )
+            for i in range(n_outer - 1)
+        ]
+        for g in range(GROUPS)
+    ]
+
+    def finish_kv(g):
+        sib[2][g].wait_recv()
+        ring[2][g].wait_recv()
+        ring[3][g].wait_recv()
+        whole = (
+            own[2, g] + sib_in[2, g].astype(F32)
+            + ring_in[2, g].astype(F32) + ring_in[3, g].astype(F32)
+        ).astype(BF16)
+        grad_kv[g, 0] = whole[:, :HEAD]
+        grad_kv[g, 1] = whole[:, HEAD:]
+        pair[g].start()
+
+    def row_first(g):
+        pair[g].wait_recv()
+        both_kv = jnp.concatenate([grad_kv[g, core], grad_kv_sib[g]], axis=0)
+        part[g] = product(rows_turned[...], both_kv, 1, 0).reshape(n_outer, n_x, 16, HEAD)
+        for i, s in enumerate(row_order):
+            row_out[g, i] = part[g, :, lax.rem(x + s, n_x)].astype(BF16)
+            row[g][i].start()
+
+    def row_last(g):
+        share = part[g, :, x]
+        for i in range(n_x - 1):
+            row[g][i].wait_recv()
+            share = share + row_in[g, i].astype(F32)
+        part[g, :, x] = share
+        col_out[g] = share.astype(BF16)
+        for copy in col[g]:
+            copy.start()
+
+    def col_last(g):
+        share = part[g, outer, x]
+        for s, copy in enumerate(col[g]):
+            copy.wait_recv()
+            share = share + col_in[g, s].astype(F32)
+        mine[0, g] = share[:8]
+        mine[1, g] = share[8:]
+
+    finish_kv(0)
     for g in range(GROUPS):
         for b in range(2):
             rows = jnp.transpose(grad_query[g, b]) * FACTOR
             for m in range(2):
                 h = g * PER_GROUP + 2 * b + m
                 dq_out[:, h * HEAD : (h + 1) * HEAD] = rows[m * TOK : (m + 1) * TOK].astype(BF16)
-    dq_store = pltpu.make_async_copy(dq_out, dq_hbm, store_sem.at[0])
-    dq_store.start()
-
-    for g in range(GROUPS):
-        sib[2][g].wait_recv()
-        ring[2][g].wait_recv()
-        ring[3][g].wait_recv()
-        grad_kv[g] = (
-            own[2, g] + sib_in[2, g].astype(F32)
-            + ring_in[2, g].astype(F32) + ring_in[3, g].astype(F32)
-        ).astype(BF16)
-    pair = remote(grad_kv.at[1 - core], grad_kv_sib, pair_send, pair_recv, sibling)
-    pair.start()
-    rows_copy.wait_recv()
-    pair.wait_recv()
-
-    def weight_rows(i, carry):
-        at = pl.ds(pl.multiple_of(i * 128, 128), 128)
-        block = product(rows_in[:, at], grad_kv[core], 0, 0)
-        block = block + product(rows_sib[:, at], grad_kv_sib[...], 0, 0)
-        for s in range(128 // (16 * n_x)):
-            start = pl.multiple_of((i * (128 // (16 * n_x)) + s) * 16, 16)
-            for to in range(n_x):
-                lo = (s * n_x + to) * 16
-                part[to, pl.ds(start, 16), :] = block[lo : lo + 16, :]
-        return carry
-
-    lax.fori_loop(0, MODEL // 128, weight_rows, 0)
-
-    rows_x = 16 * n_outer // 2
-    top, bottom = pl.ds(0, rows_x), pl.ds(rows_x, rows_x)
-    at_right, at_left = lax.rem(x + 1, n_x), lax.rem(x + n_x - 1, n_x)
-    opposite = lax.rem(x + 2, n_x)
-    row = [
-        remote(row_out.at[i], row_in.at[i], row_send.at[i], row_recv.at[i], device)
-        for i, device in enumerate(
-            [row_right, row_left, row_right, row_left, row_right, row_left]
-        )
-    ]
-    for i, (to, rows) in enumerate(
-        [(opposite, top), (opposite, bottom), (at_right, bottom), (at_left, top)]
-    ):
-        row_out[i] = part[to, rows, :].astype(BF16)
-        row[i].start()
+    row_first(0)
+    finish_kv(1)
+    row_first(1)
+    row_last(0)
     kv_rows = jnp.concatenate(
-        [grad_kv[0, :, :HEAD], grad_kv[1, :, :HEAD], grad_kv[0, :, HEAD:], grad_kv[1, :, HEAD:]],
-        axis=1,
+        [grad_kv[0, 0], grad_kv[1, 0], grad_kv[0, 1], grad_kv[1, 1]], axis=1
     )
     dx_out[...] = product(kv_rows, weight[...], 1, 1).astype(BF16)
-    dx_store = pltpu.make_async_copy(dx_out, dx_hbm, store_sem.at[1])
-    dx_store.start()
-    for i, (to, rows) in enumerate([(at_right, top), (at_left, bottom)]):
-        row[i].wait_recv()
-        row_out[4 + i] = (part[to, rows, :] + row_in[i].astype(F32)).astype(BF16)
-        row[4 + i].start()
-    for i in range(2, 6):
-        row[i].wait_recv()
-    upper = part[x, top, :] + row_in[3].astype(F32) + row_in[4].astype(F32)
-    lower = part[x, bottom, :] + row_in[2].astype(F32) + row_in[5].astype(F32)
-    part[x, top, :] = upper
-    part[x, bottom, :] = lower
-    col_out[top, :] = upper.astype(BF16)
-    col_out[bottom, :] = lower.astype(BF16)
-
-    col = []
-    for s in range(1, n_outer):
-        to = lax.rem(outer + s, n_outer)
-        copy = remote(
-            col_out.at[pl.ds(pl.multiple_of(to * 16, 16), 16)], col_in.at[s - 1],
-            col_send.at[s - 1], col_recv.at[s - 1], col_peers[s - 1],
-        )
-        copy.start()
-        col.append(copy)
-    share = part[x, pl.ds(pl.multiple_of(outer * 16, 16), 16), :]
-    for s, copy in enumerate(col):
-        copy.wait_recv()
-        share = share + col_in[s].astype(F32)
-    mine[...] = share
+    row_last(1)
+    col_last(0)
+    col_last(1)
 
     last = []
     for i, (s, flip, peer) in enumerate(dp_peers):
-        half = 1 - core if flip else core
         copy = remote(
-            mine.at[pl.ds(pl.multiple_of(half * 8, 8), 8)], dp_buf.at[dp, core],
+            mine.at[1 - core if flip else core], dp_buf.at[dp, core],
             dp_send.at[i], dp_recv.at[i], peer,
         )
         copy.start()
         last.append(copy)
-    dp_buf[dp, core] = mine[pl.ds(pl.multiple_of(core * 8, 8), 8), :]
+    dp_buf[dp, core] = mine[core]
     for copy in last:
         copy.wait_recv()
-    for g in range(GROUPS):
-        whole = dp_buf[0, g]
+    for kind in range(2):
+        whole = dp_buf[0, kind]
         for r in range(1, n_dp):
-            whole = whole + dp_buf[r, g]
-        gw_ref[:, g * HEAD : (g + 1) * HEAD] = whole[:, :HEAD]
-        gw_ref[:, (GROUPS + g) * HEAD : (GROUPS + g + 1) * HEAD] = whole[:, HEAD:]
-
-    for copy in halo + sum(sib, []) + sum(ring, []) + [rows_copy, pair] + row + col + last:
+            whole = whole + dp_buf[r, kind]
+        for g in range(GROUPS):
+            at = kind * GROUPS + g
+            gw_ref[:, at * HEAD : (at + 1) * HEAD] = whole[g]
+
+    for copy in halo + sum(sib, []) + sum(ring, []) + [rows_copy] + pair + sum(row, []) + sum(col, []) + last:
         copy.wait_send()
-    dq_store.wait()
-    dx_store.wait()
+
+
+PARTS = 4
+
+
+def place(*refs):
+    count = len(refs) // 2
+    sems = refs[-1]
+    copies = []
+    for source, target in zip(refs[:count], refs[count:-1]):
+        rows = source.shape[0] // PARTS if source.shape[0] == TOK else source.shape[0]
+        for start in range(0, source.shape[0], rows):
+            at = pl.ds(start, rows)
+            copies.append(
+                pltpu.make_async_copy(source.at[at], target.at[at], sems.at[len(copies)])
+            )
+    for copy in copies:
+        copy.start()
+    for copy in copies:
+        copy.wait()
 
 
 def on_device(sizes, queries, inputs, kv_weight, grad_out, segment_ids):
     n_dp, n_outer, n_inner = sizes
     n_x = n_inner // 2
-    rows = 16 * n_outer
     vmem, dma = pltpu.VMEM, pltpu.SemaphoreType.DMA
     anywhere = pl.BlockSpec(memory_space=pl.ANY)
     inside = pl.BlockSpec(memory_space=pltpu.VMEM)
     tokens = jax.ShapeDtypeStruct((TOK, MODEL), BF16)
-    grad_query, grad_input, grad_weight = pl.pallas_call(
+    shapes = (tokens, tokens, jax.ShapeDtypeStruct((8, WIDTH), F32))
+    results = pl.pallas_call(
         functools.partial(kernel, *sizes),
-        out_shape=(tokens, tokens, jax.ShapeDtypeStruct((8, WIDTH), F32)),
+        out_shape=tuple(pltpu.VMEM(leaf.shape, leaf.dtype) for leaf in shapes),
         in_specs=[anywhere] * 4 + [inside],
-        out_specs=(anywhere, anywhere, inside),
+        out_specs=(inside,) * 3,
         scratch_shapes=[
             vmem((2, TOK, MODEL), BF16),
             vmem((TOK, MODEL), BF16),
             vmem((TOK, MODEL), BF16),
+            vmem((MODEL, PAIR), BF16),
             vmem((MODEL, WIDTH), BF16),
             vmem((GROUPS, PER_GROUP * TOK, HEAD), BF16),
             vmem((GROUPS, PER_GROUP * TOK, HEAD), BF16),
@@ -469,26 +505,31 @@
             vmem((SPAN, GROUPS, TOK, HALF), BF16),
             vmem((4, GROUPS, TOK, HALF), BF16),
             vmem((4, GROUPS, TOK, HALF), BF16),
-            vmem((GROUPS, TOK, HALF), BF16),
-            vmem((TOK, HALF), BF16),
-            vmem((TOK, MODEL), BF16),
-            vmem((TOK, MODEL), BF16),
-            vmem((n_x, rows, HALF), F32),
-            vmem((6, rows // 2, HALF), BF16),
-            vmem((6, rows // 2, HALF), BF16),
-            vmem((rows, HALF), BF16),
-            vmem((n_outer - 1, 16, HALF), BF16),
-            vmem((16, HALF), F32),
-            vmem((n_dp, 2, 8, HALF), F32),
-            dma((4,)), dma((2,)),
+            vmem((GROUPS, 2, TOK, HEAD), BF16),
+            vmem((GROUPS, TOK, HEAD), BF16),
+            vmem((GROUPS, n_outer, n_x, 16, HEAD), F32),
+            vmem((GROUPS, n_x - 1, n_outer, 16, HEAD), BF16),
+            vmem((GROUPS, n_x - 1, n_outer, 16, HEAD), BF16),
+            vmem((GROUPS, n_outer, 16, HEAD), BF16),
+            vmem((GROUPS, n_outer - 1, 16, HEAD), BF16),
+            vmem((2, GROUPS, 8, HEAD), F32),
+            vmem((n_dp, 2, GROUPS, 8, HEAD), F32),
+            dma((4,)),
             dma((18,)), dma((18,)), dma, dma, dma((10,)), dma((10,)), dma((8,)), dma((8,)),
-            dma, dma, dma((6,)), dma((6,)),
-            dma((n_outer - 1,)), dma((n_outer - 1,)), dma((2 * n_dp - 1,)), dma((2 * n_dp - 1,)),
+            dma((2,)), dma((2,)), dma((2 * (n_x - 1),)), dma((2 * (n_x - 1),)),
+            dma((2 * (n_outer - 1),)), dma((2 * (n_outer - 1),)), dma((2 * n_dp - 1,)), dma((2 * n_dp - 1,)),
         ],
         compiler_params=pltpu.CompilerParams(
             collective_id=0, has_side_effects=True, vmem_limit_bytes=56 * 2**20
         ),
     )(queries[0], inputs[0], kv_weight, grad_out[0], segment_ids)
+    grad_query, grad_input, grad_weight = pl.pallas_call(
+        place,
+        out_shape=shapes,
+        in_specs=[inside] * 3,
+        out_specs=(anywhere,) * 3,
+        scratch_shapes=[dma((2 * PARTS + 1,))],
+    )(*results)
     return grad_query[None], grad_input[None], grad_weight
 
 

time: 73.2 us -> 70.1 us (0.958)
  Pallas kernels: 69.2 us -> 67.2 us
  local copies, waits for them, and re-layouts: 3.18 us -> 2.09 us
    pallas_call x1 -> x2, Pallas kernels: 69.2 us -> 67.2 us  [the longest x1 65.1 us: on_device(): pl.pallas_call(functools.partial(kernel, *sizes), out_shape=tuple((pltpu....]
    unnamed x7 -> x6, local copies, waits for them, and re-layouts: 3.18 us -> 2.09 us
where the time goes in v4:
time: 70.1 us; the launch traced here: 69.9 us
  Pallas kernels  67.2 us (96%)
  local copies, waits for them, and re-layouts  2.09 us (3%)
    pallas_call x1, Pallas kernels, on_device(): pl.pallas_call(functools.partial(kernel, *sizes), out_shape=tuple((pltpu....  65.1 us
    unnamed x6, local copies, waits for them, and re-layouts  2.09 us
    pallas_call x1, Pallas kernels, on_device(): pl.pallas_call(place, out_shape=shapes, in_specs=[inside] * 3, out_specs=...  2.06 us

profile of v4, /device:TPU:1, one launch (start us, length us, event | category | flops | bytes accessed | tf_op | source)
XLA Modules:
  0.0 69.9 jit_solution(5842132252453156765)
XLA Ops:
  0.6 65.1 %shard_map.76 = (bf16[192,1024]{1,0:T(8,128)(2,1)S(1)}, bf16[192,1024]{1,0:T(8,128)(2,1)S(1)}, f32[8,512]{1,0:T(8,128)S(1)}) custom-call(bf16[192,1024]{1,0:T(8,128)(2,1)} %bitcast.5, bf16[192,1024]{1,0:T(8,128)(2,1)} %bitcast.6, bf16[1024,512]{1,0:T(8,128)(2,1)} %w_hbm.1, bf16[192,1024]{1,0:T(8,128)(2,1)} %bitcast.7, s32[1,192]{1,0:T(1,128)} %ids_ref.1), custom_call_target="tpu_custom_call" | custom-call | tf_op jit(solution)/shard_map/pallas_call | solution.py:481
  65.7 0.0 copy-start
  65.8 0.7 %copy-done = bf16[192,1024]{1,0:T(8,128)(2,1)} copy-done((bf16[192,1024]{1,0:T(8,128)(2,1)}, bf16[192,1024]{1,0:T(8,128)(2,1)S(1)}, u32[]{:S(2)}) %copy-start) | copy-done | bytes 393240
  66.5 0.0 copy-start.1
  66.5 0.8 %copy-done.1 = bf16[192,1024]{1,0:T(8,128)(2,1)} copy-done((bf16[192,1024]{1,0:T(8,128)(2,1)}, bf16[192,1024]{1,0:T(8,128)(2,1)S(1)}, u32[]{:S(2)}) %copy-start.1) | copy-done | bytes 393240
  67.3 0.0 copy-start.2
  67.3 0.6 copy-done.2
  67.8 2.1 %shard_map.77 = (bf16[192,1024]{1,0:T(8,128)(2,1)}, bf16[192,1024]{1,0:T(8,128)(2,1)}, f32[8,512]{1,0:T(8,128)}) custom-call(bf16[192,1024]{1,0:T(8,128)(2,1)} %copy-done, bf16[192,1024]{1,0:T(8,128)(2,1)} %copy-done.1, f32[8,512]{1,0:T(8,128)} %copy-done.2), custom_call_target="tpu_custom_call" | custom-call | tf_op jit(solution)/shard_map/pallas_call | solution.py:526
Async XLA Ops:
  65.7 0.7 %copy-start = (bf16[192,1024]{1,0:T(8,128)(2,1)}, bf16[192,1024]{1,0:T(8,128)(2,1)S(1)}, u32[]{:S(2)}) copy-start(bf16[192,1024]{1,0:T(8,128)(2,1)S(1)} %get-tuple-element.9.refs_0_) | copy-start | bytes 1179652
  66.5 0.8 %copy-start.1 = (bf16[192,1024]{1,0:T(8,128)(2,1)}, bf16[192,1024]{1,0:T(8,128)(2,1)S(1)}, u32[]{:S(2)}) copy-start(bf16[192,1024]{1,0:T(8,128)(2,1)S(1)} %get-tuple-element.10.refs_1_) | copy-start | bytes 1179652
  67.3 0.6 copy-start.2

commit v5 on v4

--- a/solution.py
+++ b/solution.py
@@ -88,20 +88,23 @@
         for flip in (0, 1)
         if s or flip
     ]
-    peers = [right, left] + row_peers + col_peers + [peer for _, _, peer in dp_peers]
-
-    barrier = pltpu.get_barrier_semaphore()
-    for peer in peers:
-        pl.semaphore_signal(barrier, inc=1, device_id=peer, device_id_type=MESH)
-
+    peers = [peer for _, _, peer in dp_peers] + col_peers + row_peers + [right, left]
+
+    blocks = [(g + GROUPS * kind) * HEAD for g in range(GROUPS) for kind in range(2)]
     loads = [
         pltpu.make_async_copy(source, target, load_sem.at[i])
         for i, (source, target) in enumerate(
-            [(in_hbm, rows_in), (w_hbm, weight), (q_hbm, raw.at[0]), (up_hbm, raw.at[1])]
+            [(in_hbm, rows_in)]
+            + [(w_hbm.at[:, pl.ds(at, HEAD)], weight.at[:, pl.ds(at, HEAD)]) for at in blocks]
+            + [(q_hbm, raw.at[0]), (up_hbm, raw.at[1])]
         )
     ]
     for load in loads:
         load.start()
+
+    barrier = pltpu.get_barrier_semaphore()
+    for peer in peers:
+        pl.semaphore_signal(barrier, inc=1, device_id=peer, device_id_type=MESH)
 
     ids_row = ids_ref[...].astype(F32)
     twice = jnp.concatenate([ids_row, ids_row, jnp.zeros((1, 2 * HALF - PAIR), F32)], axis=1)
@@ -115,13 +118,6 @@
     loads[0].wait()
     rows_copy = remote(rows_in, rows_sib, rows_send, rows_recv, sibling)
     rows_copy.start()
-    loads[1].wait()
-    key_value = product(rows_in[...], weight[...], 1, 0).astype(BF16)
-    for g in range(GROUPS):
-        window[HERE, 0, g, 0:TOK, :HEAD] = key_value[:, g * HEAD : (g + 1) * HEAD]
-        window[HERE, 0, g, 0:TOK, HEAD:] = key_value[
-            :, (GROUPS + g) * HEAD : (GROUPS + g + 1) * HEAD
-        ]
     halo = []
     for g in range(GROUPS):
         rows = pl.ds(0, TOK if g else SENT)
@@ -146,11 +142,17 @@
                 )
             )
     for g in range(GROUPS):
+        loads[1 + 2 * g].wait()
+        loads[2 + 2 * g].wait()
+        columns = jnp.concatenate(
+            [weight[:, at : at + HEAD] for at in blocks[2 * g : 2 * g + 2]], axis=1
+        )
+        window[HERE, 0, g, 0:TOK, :] = product(rows_in[...], columns, 1, 0).astype(BF16)
         for i in (1, 2, 0):
             halo[9 * g + i].start()
 
-    loads[2].wait()
-    loads[3].wait()
+    loads[5].wait()
+    loads[6].wait()
     for h in range(HEADS):
         g, member = h // PER_GROUP, h % PER_GROUP
         at = slice(h * HEAD, (h + 1) * HEAD)
@@ -231,16 +233,11 @@
         sib_out[j, g, :, :HEAD] = key[TOK:].astype(BF16)
         sib_out[j, g, :, HEAD:] = value[TOK:].astype(BF16)
 
-    sib = [
-        [
-            remote(
-                sib_out.at[j, g], sib_in.at[j, g],
-                sib_send.at[GROUPS * j + g], sib_recv.at[GROUPS * j + g], sibling,
-            )
-            for g in range(GROUPS)
-        ]
-        for j in range(SPAN)
-    ]
+    def to_sibling(j, g):
+        at = GROUPS * j + g
+        return remote(sib_out.at[j, g], sib_in.at[j, g], sib_send.at[at], sib_recv.at[at], sibling)
+
+    sib = [[to_sibling(j, g) for g in range(GROUPS)] for j in range(SPAN)]
     ring = [
         [
             remote(
@@ -309,38 +306,43 @@
     halo[15].wait_recv()
     both(lambda j: first_pass(j, 1, False), 1, 2)
 
+    def distant(g):
+        def step(t, carry):
+            j = 4 * t
+            rows = pl.ds(0, TOK if g else SENT)
+            remote(
+                window.at[j, 0, g, rows], window.at[j, 1, g, rows],
+                halo_send.at[9 * g + 7 + t], halo_recv.at[9 * g + 7 + t], sibling,
+            ).wait_recv()
+            if not g:
+                make_mask(j)
+            first_pass(j, g, False)
+            return carry
+
+        lax.fori_loop(0, 2, step, 0)
+        merge(g)
+
+    def second_and_send(j, g):
+        second_pass(j, g, False)
+        to_sibling(j, g).start()
+
+    grad_query[...] = jnp.zeros_like(grad_query)
     distant_arrived(0)
-    halo[7].wait_recv()
-    halo[8].wait_recv()
-    both(make_mask, 0, 4)
-    both(lambda j: first_pass(j, 0, False), 0, 4)
-    merge(0)
-    grad_query[...] = jnp.zeros_like(grad_query)
+    distant(0)
     distant_arrived(1)
-    both(lambda j: second_pass(j, 0, False), 0, 4)
-    sib[0][0].start()
-    sib[4][0].start()
-    halo[16].wait_recv()
-    halo[17].wait_recv()
-    both(lambda j: first_pass(j, 1, False), 0, 4)
+    both(lambda j: second_and_send(j, 0), 0, 4)
+    distant(1)
     send_distant(0)
-    merge(1)
-    both(lambda j: second_pass(j, 1, False), 0, 4)
-    sib[0][1].start()
-    sib[4][1].start()
-    both(lambda j: second_pass(j, 0, False), 1, 2)
-    sib[1][0].start()
-    sib[3][0].start()
+    both(lambda j: second_and_send(j, 1), 0, 4)
+    second_and_send(1, 0)
     send_distant(1)
+    second_and_send(3, 0)
+    second_and_send(1, 1)
     send_near(0)
-    both(lambda j: second_pass(j, 1, False), 1, 2)
-    sib[1][1].start()
-    sib[3][1].start()
-    second_pass(HERE, 0, False)
-    sib[2][0].start()
+    second_and_send(3, 1)
+    second_and_send(HERE, 0)
     send_near(1)
-    second_pass(HERE, 1, False)
-    sib[2][1].start()
+    second_and_send(HERE, 1)
 
     pair = [
         remote(
@@ -514,7 +516,7 @@
             vmem((GROUPS, n_outer - 1, 16, HEAD), BF16),
             vmem((2, GROUPS, 8, HEAD), F32),
             vmem((n_dp, 2, GROUPS, 8, HEAD), F32),
-            dma((4,)),
+            dma((7,)),
             dma((18,)), dma((18,)), dma, dma, dma((10,)), dma((10,)), dma((8,)), dma((8,)),
             dma((2,)), dma((2,)), dma((2 * (n_x - 1),)), dma((2 * (n_x - 1),)),
             dma((2 * (n_outer - 1),)), dma((2 * (n_outer - 1),)), dma((2 * n_dp - 1,)), dma((2 * n_dp - 1,)),

time: 70.1 us -> 68.5 us (0.977)
  Pallas kernels: 67.2 us -> 65.6 us
    pallas_call x1, Pallas kernels: 65.1 us -> 63.6 us  [on_device(): pl.pallas_call(functools.partial(kernel, *sizes), out_shape=tuple((pltpu....]
where the time goes in v5:
time: 68.5 us; the launch traced here: 68.4 us
  Pallas kernels  65.6 us (96%)
  local copies, waits for them, and re-layouts  2.09 us (3%)
    pallas_call x1, Pallas kernels, on_device(): pl.pallas_call(functools.partial(kernel, *sizes), out_shape=tuple((pltpu....  63.6 us
    unnamed x6, local copies, waits for them, and re-layouts  2.09 us
    pallas_call x1, Pallas kernels, on_device(): pl.pallas_call(place, out_shape=shapes, in_specs=[inside] * 3, out_specs=...  2.06 us

profile of v5, /device:TPU:1, one launch (start us, length us, event | category | flops | bytes accessed | tf_op | source)
XLA Modules:
  0.0 68.4 jit_solution(7759931841399962030)
XLA Ops:
  0.6 63.6 %shard_map.76 = (bf16[192,1024]{1,0:T(8,128)(2,1)S(1)}, bf16[192,1024]{1,0:T(8,128)(2,1)S(1)}, f32[8,512]{1,0:T(8,128)S(1)}) custom-call(bf16[192,1024]{1,0:T(8,128)(2,1)} %bitcast.5, bf16[192,1024]{1,0:T(8,128)(2,1)} %bitcast.6, bf16[1024,512]{1,0:T(8,128)(2,1)} %w_hbm.1, bf16[192,1024]{1,0:T(8,128)(2,1)} %bitcast.7, s32[1,192]{1,0:T(1,128)} %ids_ref.1), custom_call_target="tpu_custom_call" | custom-call | tf_op jit(solution)/shard_map/pallas_call | solution.py:483
  64.2 0.0 copy-start
  64.2 0.7 %copy-done = bf16[192,1024]{1,0:T(8,128)(2,1)} copy-done((bf16[192,1024]{1,0:T(8,128)(2,1)}, bf16[192,1024]{1,0:T(8,128)(2,1)S(1)}, u32[]{:S(2)}) %copy-start) | copy-done | bytes 393240
  65.0 0.0 copy-start.1
  65.0 0.8 %copy-done.1 = bf16[192,1024]{1,0:T(8,128)(2,1)} copy-done((bf16[192,1024]{1,0:T(8,128)(2,1)}, bf16[192,1024]{1,0:T(8,128)(2,1)S(1)}, u32[]{:S(2)}) %copy-start.1) | copy-done | bytes 393240
  65.7 0.0 copy-start.2
  65.7 0.6 copy-done.2
  66.3 2.1 %shard_map.77 = (bf16[192,1024]{1,0:T(8,128)(2,1)}, bf16[192,1024]{1,0:T(8,128)(2,1)}, f32[8,512]{1,0:T(8,128)}) custom-call(bf16[192,1024]{1,0:T(8,128)(2,1)} %copy-done, bf16[192,1024]{1,0:T(8,128)(2,1)} %copy-done.1, f32[8,512]{1,0:T(8,128)} %copy-done.2), custom_call_target="tpu_custom_call" | custom-call | tf_op jit(solution)/shard_map/pallas_call | solution.py:528
Async XLA Ops:
  64.2 0.7 %copy-start = (bf16[192,1024]{1,0:T(8,128)(2,1)}, bf16[192,1024]{1,0:T(8,128)(2,1)S(1)}, u32[]{:S(2)}) copy-start(bf16[192,1024]{1,0:T(8,128)(2,1)S(1)} %get-tuple-element.9.refs_0_) | copy-start | bytes 1179652
  65.0 0.8 %copy-start.1 = (bf16[192,1024]{1,0:T(8,128)(2,1)}, bf16[192,1024]{1,0:T(8,128)(2,1)S(1)}, u32[]{:S(2)}) copy-start(bf16[192,1024]{1,0:T(8,128)(2,1)S(1)} %get-tuple-element.10.refs_1_) | copy-start | bytes 1179652
  65.7 0.6 copy-start.2

commit v6 on v5

--- a/solution.py
+++ b/solution.py
@@ -52,10 +52,11 @@
     dq_out, dx_out, gw_ref,
     raw, rows_in, rows_sib, rows_turned, weight, queries, upstream,
     window, ids_query, mask, scores, grads, peak, total, dots, grad_query,
-    own, sib_out, sib_in, ring_out, ring_in, grad_kv, grad_kv_sib,
+    own, sib_out, sib_in, here_out, far_out, far_in, near_out, near_in, kv_pair, kv_own,
     part, row_out, row_in, col_out, col_in, mine, dp_buf,
     load_sem,
-    halo_send, halo_recv, rows_send, rows_recv, sib_send, sib_recv, ring_send, ring_recv,
+    halo_send, halo_recv, rows_send, rows_recv, sib_send, sib_recv,
+    far_send, far_recv, near_send, near_recv,
     pair_send, pair_recv, row_send, row_recv, col_send, col_recv, dp_send, dp_recv,
 ):
     n_x = n_inner // 2
@@ -66,12 +67,13 @@
     x, core = inner // 2, inner % 2
     chip = outer * n_x + x
 
-    def chip_at(steps):
+    def chip_at(steps, at_core):
         there = lax.rem(chip + steps + chips, chips)
-        return (dp, there // n_x, lax.rem(there, n_x) * 2 + core)
+        return (dp, there // n_x, lax.rem(there, n_x) * 2 + at_core)
 
     sibling = (dp, outer, x * 2 + 1 - core)
-    right, left = chip_at(1), chip_at(-1)
+    right, left = chip_at(1, core), chip_at(-1, core)
+    across = [chip_at(1, 1 - core), chip_at(-1, 1 - core)]
     row_order = sorted(range(1, n_x), key=lambda s: -min(s, n_x - s))
     row_peers = [(dp, outer, lax.rem(x + s, n_x) * 2 + core) for s in row_order]
     n_y = n_outer // 2
@@ -88,7 +90,7 @@
         for flip in (0, 1)
         if s or flip
     ]
-    peers = [peer for _, _, peer in dp_peers] + col_peers + row_peers + [right, left]
+    peers = [peer for _, _, peer in dp_peers] + col_peers + row_peers + across + [right, left]
 
     blocks = [(g + GROUPS * kind) * HEAD for g in range(GROUPS) for kind in range(2)]
     loads = [
@@ -228,25 +230,54 @@
             query = product(keys, grad, 0, 0)
             grad_query[g, b] = query if opening else grad_query[g, b] + query
         key = key * FACTOR
-        own[j, g, :, :HEAD] = key[:TOK]
-        own[j, g, :, HEAD:] = value[:TOK]
-        sib_out[j, g, :, :HEAD] = key[TOK:].astype(BF16)
-        sib_out[j, g, :, HEAD:] = value[TOK:].astype(BF16)
+        own[j, g, 0] = key[:TOK]
+        own[j, g, 1] = value[:TOK]
+        sib_out[j, g, 0] = key[TOK:].astype(BF16)
+        sib_out[j, g, 1] = value[TOK:].astype(BF16)
 
     def to_sibling(j, g):
         at = GROUPS * j + g
         return remote(sib_out.at[j, g], sib_in.at[j, g], sib_send.at[at], sib_recv.at[at], sibling)
 
     sib = [[to_sibling(j, g) for g in range(GROUPS)] for j in range(SPAN)]
-    ring = [
+    far = [
         [
-            remote(
-                ring_out.at[i, g], ring_in.at[i, g],
-                ring_send.at[GROUPS * i + g], ring_recv.at[GROUPS * i + g], device,
-            )
+            [
+                remote(
+                    far_out.at[i, g, kind], far_in.at[i, g, kind],
+                    far_send.at[4 * i + 2 * g + kind], far_recv.at[4 * i + 2 * g + kind], device,
+                )
+                for kind in range(2)
+            ]
             for g in range(GROUPS)
         ]
-        for i, device in enumerate([left, right, left, right])
+        for i, device in enumerate([left, right])
+    ]
+
+    def to_neighbour(i, g, kind):
+        side = lax.rem(core + kind, 2)
+        return remote(
+            near_out.at[i, g, kind], near_in.at[i, g, side],
+            near_send.at[4 * i + 2 * g + kind], near_recv.at[4 * i + 2 * g + side],
+            chip_at(2 * i - 1, kind),
+        )
+
+    near = [
+        [[to_neighbour(i, g, kind) for kind in range(2)] for g in range(GROUPS)] for i in range(2)
+    ]
+    here = [
+        remote(
+            here_out.at[g], sib_in.at[HERE, g],
+            sib_send.at[GROUPS * HERE + g], sib_recv.at[GROUPS * HERE + g], sibling,
+        )
+        for g in range(GROUPS)
+    ]
+    swap = [
+        remote(
+            kv_pair.at[g, pl.ds(TOK, TOK)], kv_own.at[core, g],
+            pair_send.at[g], pair_recv.at[g], sibling,
+        )
+        for g in range(GROUPS)
     ]
 
     def turn_inputs():
@@ -277,17 +308,29 @@
     def send_distant(g):
         for i, j in enumerate((0, 4)):
             sib[j][g].wait_recv()
-            ring_out[i, g] = (own[j, g] + sib_in[j, g].astype(F32)).astype(BF16)
-            ring[i][g].start()
+            for kind in range(2):
+                far_out[i, g, kind] = (
+                    own[j, g, kind] + sib_in[j, g, kind].astype(F32)
+                ).astype(BF16)
+                far[i][g][kind].start()
 
     def send_near(g):
         for i, j in enumerate((1, 3)):
             sib[j][g].wait_recv()
-            ring[i][g].wait_recv()
-            ring_out[2 + i, g] = (
-                own[j, g] + sib_in[j, g].astype(F32) + ring_in[i, g].astype(F32)
-            ).astype(BF16)
-            ring[2 + i][g].start()
+        for kind in range(2):
+            for i, j in enumerate((1, 3)):
+                far[i][g][kind].wait_recv()
+                near_out[i, g, kind] = (
+                    own[j, g, kind] + sib_in[j, g, kind].astype(F32)
+                    + far_in[i, g, kind].astype(F32)
+                ).astype(BF16)
+                near[i][g][kind].start()
+
+    def send_here(g):
+        second_pass(HERE, g, False)
+        here_out[g, 0] = own[HERE, g, 1 - core].astype(BF16)
+        here_out[g, 1] = sib_out[HERE, g, 1 - core]
+        here[g].start()
 
     halo[0].wait_recv()
     make_mask(HERE)
@@ -340,16 +383,10 @@
     second_and_send(1, 1)
     send_near(0)
     second_and_send(3, 1)
-    second_and_send(HERE, 0)
+    send_here(0)
     send_near(1)
-    second_and_send(HERE, 1)
-
-    pair = [
-        remote(
-            grad_kv.at[g, 1 - core], grad_kv_sib.at[g], pair_send.at[g], pair_recv.at[g], sibling
-        )
-        for g in range(GROUPS)
-    ]
+    send_here(1)
+
     row = [
         [
             remote(
@@ -373,21 +410,27 @@
     ]
 
     def finish_kv(g):
-        sib[2][g].wait_recv()
-        ring[2][g].wait_recv()
-        ring[3][g].wait_recv()
-        whole = (
-            own[2, g] + sib_in[2, g].astype(F32)
-            + ring_in[2, g].astype(F32) + ring_in[3, g].astype(F32)
-        ).astype(BF16)
-        grad_kv[g, 0] = whole[:, :HEAD]
-        grad_kv[g, 1] = whole[:, HEAD:]
-        pair[g].start()
+        here[g].wait_recv()
+        for i in range(2):
+            for side in range(2):
+                remote(
+                    near_out.at[i, g, side], near_in.at[i, g, side],
+                    near_send.at[4 * i + 2 * g + side], near_recv.at[4 * i + 2 * g + side], right,
+                ).wait_recv()
+        mine_kv = own[HERE, g, core] + sib_in[HERE, g, 1].astype(F32)
+        sib_kv = sib_out[HERE, g, core].astype(F32) + sib_in[HERE, g, 0].astype(F32)
+        for i in range(2):
+            mine_kv = mine_kv + near_in[i, g, 0].astype(F32)
+            sib_kv = sib_kv + near_in[i, g, 1].astype(F32)
+        mine_kv = mine_kv.astype(BF16)
+        kv_own[core, g] = mine_kv
+        kv_pair[g, 0:TOK, :] = mine_kv
+        kv_pair[g, TOK:PAIR, :] = sib_kv.astype(BF16)
+        swap[g].start()
 
     def row_first(g):
-        pair[g].wait_recv()
-        both_kv = jnp.concatenate([grad_kv[g, core], grad_kv_sib[g]], axis=0)
-        part[g] = product(rows_turned[...], both_kv, 1, 0).reshape(n_outer, n_x, 16, HEAD)
+        whole = product(rows_turned[...], kv_pair[g], 1, 0)
+        part[g] = whole.reshape(n_outer, n_x, 16, HEAD)
         for i, s in enumerate(row_order):
             row_out[g, i] = part[g, :, lax.rem(x + s, n_x)].astype(BF16)
             row[g][i].start()
@@ -421,8 +464,10 @@
     finish_kv(1)
     row_first(1)
     row_last(0)
+    for g in range(GROUPS):
+        swap[g].wait_recv()
     kv_rows = jnp.concatenate(
-        [grad_kv[0, 0], grad_kv[1, 0], grad_kv[0, 1], grad_kv[1, 1]], axis=1
+        [kv_own[kind, g] for kind in range(2) for g in range(GROUPS)], axis=1
     )
     dx_out[...] = product(kv_rows, weight[...], 1, 1).astype(BF16)
     row_last(1)
@@ -448,7 +493,9 @@
             at = kind * GROUPS + g
             gw_ref[:, at * HEAD : (at + 1) * HEAD] = whole[g]
 
-    for copy in halo + sum(sib, []) + sum(ring, []) + [rows_copy] + pair + sum(row, []) + sum(col, []) + last:
+    others = [copy for j in range(SPAN) if j != HERE for copy in sib[j]]
+    by_kind = [copy for group in far + near for kinds in group for copy in kinds]
+    for copy in halo + others + by_kind + here + swap + [rows_copy] + sum(row + col, []) + last:
         copy.wait_send()
 
 
@@ -502,13 +549,16 @@
             vmem((GROUPS, 2, 8, PAIR), F32),
             vmem((GROUPS, 2, 8, PAIR), F32),
             vmem((GROUPS, 2, HEAD, PAIR), F32),
-            vmem((SPAN, GROUPS, TOK, HALF), F32),
-            vmem((SPAN, GROUPS, TOK, HALF), BF16),
-            vmem((SPAN, GROUPS, TOK, HALF), BF16),
-            vmem((4, GROUPS, TOK, HALF), BF16),
-            vmem((4, GROUPS, TOK, HALF), BF16),
+            vmem((SPAN, GROUPS, 2, TOK, HEAD), F32),
+            vmem((SPAN, GROUPS, 2, TOK, HEAD), BF16),
+            vmem((SPAN, GROUPS, 2, TOK, HEAD), BF16),
             vmem((GROUPS, 2, TOK, HEAD), BF16),
-            vmem((GROUPS, TOK, HEAD), BF16),
+            vmem((2, GROUPS, 2, TOK, HEAD), BF16),
+            vmem((2, GROUPS, 2, TOK, HEAD), BF16),
+            vmem((2, GROUPS, 2, TOK, HEAD), BF16),
+            vmem((2, GROUPS, 2, TOK, HEAD), BF16),
+            vmem((GROUPS, PAIR, HEAD), BF16),
+            vmem((2, GROUPS, TOK, HEAD), BF16),
             vmem((GROUPS, n_outer, n_x, 16, HEAD), F32),
             vmem((GROUPS, n_x - 1, n_outer, 16, HEAD), BF16),
             vmem((GROUPS, n_x - 1, n_outer, 16, HEAD), BF16),
@@ -517,7 +567,8 @@
             vmem((2, GROUPS, 8, HEAD), F32),
             vmem((n_dp, 2, GROUPS, 8, HEAD), F32),
             dma((7,)),
-            dma((18,)), dma((18,)), dma, dma, dma((10,)), dma((10,)), dma((8,)), dma((8,)),
+            dma((18,)), dma((18,)), dma, dma, dma((10,)), dma((10,)),
+            dma((8,)), dma((8,)), dma((8,)), dma((8,)),
             dma((2,)), dma((2,)), dma((2 * (n_x - 1),)), dma((2 * (n_x - 1),)),
             dma((2 * (n_outer - 1),)), dma((2 * (n_outer - 1),)), dma((2 * n_dp - 1,)), dma((2 * n_dp - 1,)),
         ],

time: 68.5 us -> 67.6 us (0.987)
  Pallas kernels: 65.6 us -> 64.7 us
    pallas_call x1, Pallas kernels: 63.6 us -> 62.6 us  [on_device(): pl.pallas_call(functools.partial(kernel, *sizes), out_shape=tuple((pltpu....]
where the time goes in v6:
time: 67.6 us; the launch traced here: 67.4 us
  Pallas kernels  64.7 us (96%)
  local copies, waits for them, and re-layouts  2.09 us (3%)
    pallas_call x1, Pallas kernels, on_device(): pl.pallas_call(functools.partial(kernel, *sizes), out_shape=tuple((pltpu....  62.6 us
    unnamed x6, local copies, waits for them, and re-layouts  2.09 us
    pallas_call x1, Pallas kernels, on_device(): pl.pallas_call(place, out_shape=shapes, in_specs=[inside] * 3, out_specs=...  2.06 us

profile of v6, /device:TPU:1, one launch (start us, length us, event | category | flops | bytes accessed | tf_op | source)
XLA Modules:
  0.0 67.4 jit_solution(14249163583590127119)
XLA Ops:
  0.6 62.6 %shard_map.76 = (bf16[192,1024]{1,0:T(8,128)(2,1)S(1)}, bf16[192,1024]{1,0:T(8,128)(2,1)S(1)}, f32[8,512]{1,0:T(8,128)S(1)}) custom-call(bf16[192,1024]{1,0:T(8,128)(2,1)} %bitcast.5, bf16[192,1024]{1,0:T(8,128)(2,1)} %bitcast.6, bf16[1024,512]{1,0:T(8,128)(2,1)} %w_hbm.1, bf16[192,1024]{1,0:T(8,128)(2,1)} %bitcast.7, s32[1,192]{1,0:T(1,128)} %ids_ref.1), custom_call_target="tpu_custom_call" | custom-call | tf_op jit(solution)/shard_map/pallas_call | solution.py:530
  63.3 0.0 copy-start
  63.3 0.7 %copy-done = bf16[192,1024]{1,0:T(8,128)(2,1)} copy-done((bf16[192,1024]{1,0:T(8,128)(2,1)}, bf16[192,1024]{1,0:T(8,128)(2,1)S(1)}, u32[]{:S(2)}) %copy-start) | copy-done | bytes 393240
  64.0 0.0 copy-start.1
  64.0 0.8 %copy-done.1 = bf16[192,1024]{1,0:T(8,128)(2,1)} copy-done((bf16[192,1024]{1,0:T(8,128)(2,1)}, bf16[192,1024]{1,0:T(8,128)(2,1)S(1)}, u32[]{:S(2)}) %copy-start.1) | copy-done | bytes 393240
  64.8 0.0 copy-start.2
  64.8 0.6 copy-done.2
  65.4 2.1 %shard_map.77 = (bf16[192,1024]{1,0:T(8,128)(2,1)}, bf16[192,1024]{1,0:T(8,128)(2,1)}, f32[8,512]{1,0:T(8,128)}) custom-call(bf16[192,1024]{1,0:T(8,128)(2,1)} %copy-done, bf16[192,1024]{1,0:T(8,128)(2,1)} %copy-done.1, f32[8,512]{1,0:T(8,128)} %copy-done.2), custom_call_target="tpu_custom_call" | custom-call | tf_op jit(solution)/shard_map/pallas_call | solution.py:579
Async XLA Ops:
  63.3 0.7 %copy-start = (bf16[192,1024]{1,0:T(8,128)(2,1)}, bf16[192,1024]{1,0:T(8,128)(2,1)S(1)}, u32[]{:S(2)}) copy-start(bf16[192,1024]{1,0:T(8,128)(2,1)S(1)} %get-tuple-element.9.refs_0_) | copy-start | bytes 1179652
  64.0 0.8 %copy-start.1 = (bf16[192,1024]{1,0:T(8,128)(2,1)}, bf16[192,1024]{1,0:T(8,128)(2,1)S(1)}, u32[]{:S(2)}) copy-start(bf16[192,1024]{1,0:T(8,128)(2,1)S(1)} %get-tuple-element.10.refs_1_) | copy-start | bytes 1179652
  64.8 0.6 copy-start.2

commit v7 on v6

--- a/solution.py
+++ b/solution.py
@@ -17,7 +17,6 @@
 PAIR = 2 * TOK
 SENT = TOK + 16
 HALF = 2 * HEAD
-TILES = PAIR // 8
 WIDTH = 2 * GROUPS * HEAD
 MODEL = HEADS * HEAD
 SPAN = 5
@@ -120,6 +119,8 @@
     loads[0].wait()
     rows_copy = remote(rows_in, rows_sib, rows_send, rows_recv, sibling)
     rows_copy.start()
+    far_whole, far_half = 4 * core, 4 * (1 - core)
+
     halo = []
     for g in range(GROUPS):
         rows = pl.ds(0, TOK if g else SENT)
@@ -132,15 +133,14 @@
                 ((3, 0), (4, 0), left),
                 ((1, 0), (1, 1), sibling),
                 ((3, 0), (3, 1), sibling),
-                ((0, 0), (0, 1), sibling),
-                ((4, 0), (4, 1), sibling),
+                ((far_half, 0), (far_half, 1), sibling),
             ]
         ):
             halo.append(
                 remote(
                     window.at[source[0], source[1], g, rows],
                     window.at[target[0], target[1], g, rows],
-                    halo_send.at[9 * g + i], halo_recv.at[9 * g + i], device,
+                    halo_send.at[8 * g + i], halo_recv.at[8 * g + i], device,
                 )
             )
     for g in range(GROUPS):
@@ -151,7 +151,7 @@
         )
         window[HERE, 0, g, 0:TOK, :] = product(rows_in[...], columns, 1, 0).astype(BF16)
         for i in (1, 2, 0):
-            halo[9 * g + i].start()
+            halo[8 * g + i].start()
 
     loads[5].wait()
     loads[6].wait()
@@ -161,36 +161,45 @@
         queries[g, member * TOK : (member + 1) * TOK, :] = raw[0, :, at]
         upstream[g, member * TOK : (member + 1) * TOK, :] = raw[1, :, at]
 
-    def of_chunk(j, g, at):
+    def of_chunk(j, g, at, whole=True):
+        if not whole:
+            return window[j, 0, g, 0:TOK, at]
         return jnp.concatenate([window[j, 0, g, 0:TOK, at], window[j, 1, g, 0:TOK, at]], axis=0)
 
     keys_at, values_at = slice(0, HEAD), slice(HEAD, HALF)
 
-    def make_mask(j):
+    def make_mask(j, whole=True):
+        count = PAIR if whole else TOK
         lane = lax.broadcasted_iota(jnp.int32, (1, PAIR), 1)
         near, far = (
             jnp.concatenate([ids[0:1], ids[1:2, : PAIR - HALF]], axis=1)
-            for ids in (window[j, side, 0, TOK:SENT, :].astype(F32) for side in (0, 1))
+            for ids in (
+                window[j, side, 0, TOK:SENT, :].astype(F32) for side in (0, 1 if whole else 0)
+            )
         )
         ids_key = jnp.where(lane < TOK, near, far)
         ids_col = jnp.transpose(jnp.broadcast_to(ids_key, (HEAD, PAIR)))
-        mask[j] = jnp.where(thrice(ids_col) == ids_query[0:1, :], 0.0, FAR)
-
-    def first_pass(j, g, opening):
-        keys, values = of_chunk(j, g, keys_at), of_chunk(j, g, values_at)
+        mask[j, 0:count, :] = jnp.where(
+            thrice(ids_col[:count]) == ids_query[0:1, :], 0.0, FAR
+        )
+
+    def first_pass(j, g, opening, whole=True):
+        count = PAIR if whole else TOK
+        keys, values = of_chunk(j, g, keys_at, whole), of_chunk(j, g, values_at, whole)
         for b in range(2):
             at = slice(b * PAIR, (b + 1) * PAIR)
-            score = product(keys, queries[g, at, :], 1, 1) * (FACTOR * LOG2E) + mask[j]
+            score = product(keys, queries[g, at, :], 1, 1) * (FACTOR * LOG2E)
+            score = score + mask[j, 0:count, :]
             grad = product(values, upstream[g, at, :], 1, 1)
-            scores[j, g, b] = score
-            grads[j, g, b] = grad
-            score = score.reshape(TILES, 8, PAIR)
+            scores[j, g, b, 0:count, :] = score
+            grads[j, g, b, 0:count, :] = grad
+            score = score.reshape(count // 8, 8, PAIR)
             top = jnp.max(score, axis=0)
             if not opening:
                 before = peak[g, b]
                 top = jnp.maximum(before, top)
             weights = jnp.exp2(score - top[None])
-            dot = jnp.sum(weights * grad.reshape(TILES, 8, PAIR), axis=0)
+            dot = jnp.sum(weights * grad.reshape(count // 8, 8, PAIR), axis=0)
             weights = jnp.sum(weights, axis=0)
             if not opening:
                 scale = jnp.exp2(before - top)
@@ -216,15 +225,18 @@
             peak[g, b] = jnp.broadcast_to(top + jnp.log(weights) * LOG2E, (8, PAIR))
             dots[g, b] = jnp.broadcast_to(dot, (8, PAIR))
 
-    def second_pass(j, g, opening):
-        keys = of_chunk(j, g, keys_at)
+    def second_pass(j, g, opening, whole=True):
+        count = PAIR if whole else TOK
+        keys = of_chunk(j, g, keys_at, whole)
         key, value = 0.0, 0.0
         for b in range(2):
             at = slice(b * PAIR, (b + 1) * PAIR)
-            probs = jnp.exp2(scores[j, g, b].reshape(TILES, 8, PAIR) - peak[g, b][None])
-            low = probs.reshape(PAIR, PAIR).astype(BF16)
-            grad = probs * (grads[j, g, b].reshape(TILES, 8, PAIR) - dots[g, b][None])
-            grad = grad.reshape(PAIR, PAIR).astype(BF16)
+            score = scores[j, g, b, 0:count, :].reshape(count // 8, 8, PAIR)
+            probs = jnp.exp2(score - peak[g, b][None])
+            low = probs.reshape(count, PAIR).astype(BF16)
+            grad = grads[j, g, b, 0:count, :].reshape(count // 8, 8, PAIR)
+            grad = probs * (grad - dots[g, b][None])
+            grad = grad.reshape(count, PAIR).astype(BF16)
             key = key + product(grad, queries[g, at, :], 1, 0)
             value = value + product(low, upstream[g, at, :], 1, 0)
             query = product(keys, grad, 0, 0)
@@ -232,26 +244,24 @@
         key = key * FACTOR
         own[j, g, 0] = key[:TOK]
         own[j, g, 1] = value[:TOK]
-        sib_out[j, g, 0] = key[TOK:].astype(BF16)
-        sib_out[j, g, 1] = value[TOK:].astype(BF16)
+        if whole:
+            sib_out[j, g, 0] = key[TOK:].astype(BF16)
+            sib_out[j, g, 1] = value[TOK:].astype(BF16)
 
     def to_sibling(j, g):
         at = GROUPS * j + g
         return remote(sib_out.at[j, g], sib_in.at[j, g], sib_send.at[at], sib_recv.at[at], sibling)
 
-    sib = [[to_sibling(j, g) for g in range(GROUPS)] for j in range(SPAN)]
+    sib = {j: [to_sibling(j, g) for g in range(GROUPS)] for j in (1, 3)}
+    def far_copy(i, g, kind):
+        at = 4 * i + 2 * g + kind
+        return remote(
+            far_out.at[i, g, kind], far_in.at[i, g, kind], far_send.at[at], far_recv.at[at],
+            chip_at(2 * i - 1, core),
+        )
+
     far = [
-        [
-            [
-                remote(
-                    far_out.at[i, g, kind], far_in.at[i, g, kind],
-                    far_send.at[4 * i + 2 * g + kind], far_recv.at[4 * i + 2 * g + kind], device,
-                )
-                for kind in range(2)
-            ]
-            for g in range(GROUPS)
-        ]
-        for i, device in enumerate([left, right])
+        [[far_copy(i, g, kind) for kind in range(2)] for g in range(GROUPS)] for i in range(2)
     ]
 
     def to_neighbour(i, g, kind):
@@ -292,27 +302,32 @@
         lax.fori_loop(0, MODEL // 128, turn, 0)
 
     def near_arrived(g):
-        halo[9 * g + 1].wait_recv()
-        halo[9 * g + 3].start()
-        halo[9 * g + 2].wait_recv()
-        halo[9 * g + 4].start()
-        halo[9 * g + 5].start()
-        halo[9 * g + 6].start()
+        halo[8 * g + 1].wait_recv()
+        halo[8 * g + 3].start()
+        halo[8 * g + 2].wait_recv()
+        halo[8 * g + 4].start()
+        halo[8 * g + 5].start()
+        halo[8 * g + 6].start()
 
     def distant_arrived(g):
-        halo[9 * g + 3].wait_recv()
-        halo[9 * g + 7].start()
-        halo[9 * g + 4].wait_recv()
-        halo[9 * g + 8].start()
-
-    def send_distant(g):
-        for i, j in enumerate((0, 4)):
-            sib[j][g].wait_recv()
-            for kind in range(2):
-                far_out[i, g, kind] = (
-                    own[j, g, kind] + sib_in[j, g, kind].astype(F32)
-                ).astype(BF16)
-                far[i][g][kind].start()
+        halo[8 * g + 3].wait_recv()
+        halo[8 * g + 4].wait_recv()
+        halo[8 * g + 7].start()
+
+    def send_whole(g):
+        second_pass(far_whole, g, False)
+        to_sibling(far_whole, g).start()
+        for kind in range(2):
+            far_out[core, g, kind] = own[far_whole, g, kind].astype(BF16)
+            far_copy(core, g, kind).start()
+
+    def send_half(g):
+        to_sibling(far_half, g).wait_recv()
+        for kind in range(2):
+            far_out[1 - core, g, kind] = (
+                own[far_half, g, kind] + sib_in[far_half, g, kind].astype(F32)
+            ).astype(BF16)
+            far_copy(1 - core, g, kind).start()
 
     def send_near(g):
         for i, j in enumerate((1, 3)):
@@ -335,7 +350,7 @@
     halo[0].wait_recv()
     make_mask(HERE)
     first_pass(HERE, 0, True)
-    halo[9].wait_recv()
+    halo[8].wait_recv()
     first_pass(HERE, 1, True)
 
     turn_inputs()
@@ -345,24 +360,18 @@
     both(make_mask, 1, 2)
     both(lambda j: first_pass(j, 0, False), 1, 2)
     near_arrived(1)
+    halo[13].wait_recv()
     halo[14].wait_recv()
-    halo[15].wait_recv()
     both(lambda j: first_pass(j, 1, False), 1, 2)
 
     def distant(g):
-        def step(t, carry):
-            j = 4 * t
-            rows = pl.ds(0, TOK if g else SENT)
-            remote(
-                window.at[j, 0, g, rows], window.at[j, 1, g, rows],
-                halo_send.at[9 * g + 7 + t], halo_recv.at[9 * g + 7 + t], sibling,
-            ).wait_recv()
-            if not g:
-                make_mask(j)
-            first_pass(j, g, False)
-            return carry
-
-        lax.fori_loop(0, 2, step, 0)
+        if not g:
+            make_mask(far_half, False)
+        first_pass(far_half, g, False, False)
+        halo[8 * g + 7].wait_recv()
+        if not g:
+            make_mask(far_whole)
+        first_pass(far_whole, g, False)
         merge(g)
 
     def second_and_send(j, g):
@@ -373,12 +382,14 @@
     distant_arrived(0)
     distant(0)
     distant_arrived(1)
-    both(lambda j: second_and_send(j, 0), 0, 4)
+    send_whole(0)
+    second_pass(far_half, 0, False, False)
+    send_half(0)
     distant(1)
-    send_distant(0)
-    both(lambda j: second_and_send(j, 1), 0, 4)
+    send_whole(1)
+    second_pass(far_half, 1, False, False)
     second_and_send(1, 0)
-    send_distant(1)
+    send_half(1)
     second_and_send(3, 0)
     second_and_send(1, 1)
     send_near(0)
@@ -493,7 +504,7 @@
             at = kind * GROUPS + g
             gw_ref[:, at * HEAD : (at + 1) * HEAD] = whole[g]
 
-    others = [copy for j in range(SPAN) if j != HERE for copy in sib[j]]
+    others = [to_sibling(far_whole, g) for g in range(GROUPS)] + sib[1] + sib[3]
     by_kind = [copy for group in far + near for kinds in group for copy in kinds]
     for copy in halo + others + by_kind + here + swap + [rows_copy] + sum(row + col, []) + last:
         copy.wait_send()
@@ -567,7 +578,7 @@
             vmem((2, GROUPS, 8, HEAD), F32),
             vmem((n_dp, 2, GROUPS, 8, HEAD), F32),
             dma((7,)),
-            dma((18,)), dma((18,)), dma, dma, dma((10,)), dma((10,)),
+            dma((16,)), dma((16,)), dma, dma, dma((10,)), dma((10,)),
             dma((8,)), dma((8,)), dma((8,)), dma((8,)),
             dma((2,)), dma((2,)), dma((2 * (n_x - 1),)), dma((2 * (n_x - 1),)),
             dma((2 * (n_outer - 1),)), dma((2 * (n_outer - 1),)), dma((2 * n_dp - 1,)), dma((2 * n_dp - 1,)),

time: 67.6 us -> 66.4 us (0.982)
  Pallas kernels: 64.7 us -> 63.5 us
    pallas_call x1, Pallas kernels: 62.6 us -> 61.4 us  [on_device(): pl.pallas_call(functools.partial(kernel, *sizes), out_shape=tuple((pltpu....]
where the time goes in v7:
time: 66.4 us; the launch traced here: 66.2 us
  Pallas kernels  63.5 us (96%)
  local copies, waits for them, and re-layouts  2.09 us (3%)
    pallas_call x1, Pallas kernels, on_device(): pl.pallas_call(functools.partial(kernel, *sizes), out_shape=tuple((pltpu....  61.4 us
    unnamed x6, local copies, waits for them, and re-layouts  2.09 us
    pallas_call x1, Pallas kernels, on_device(): pl.pallas_call(place, out_shape=shapes, in_specs=[inside] * 3, out_specs=...  2.06 us

profile of v7, /device:TPU:1, one launch (start us, length us, event | category | flops | bytes accessed | tf_op | source)
XLA Modules:
  0.0 66.2 jit_solution(17927661902886541920)
XLA Ops:
  0.6 61.4 %shard_map.76 = (bf16[192,1024]{1,0:T(8,128)(2,1)S(1)}, bf16[192,1024]{1,0:T(8,128)(2,1)S(1)}, f32[8,512]{1,0:T(8,128)S(1)}) custom-call(bf16[192,1024]{1,0:T(8,128)(2,1)} %bitcast.5, bf16[192,1024]{1,0:T(8,128)(2,1)} %bitcast.6, bf16[1024,512]{1,0:T(8,128)(2,1)} %w_hbm.1, bf16[192,1024]{1,0:T(8,128)(2,1)} %bitcast.7, s32[1,192]{1,0:T(1,128)} %ids_ref.1), custom_call_target="tpu_custom_call" | custom-call | tf_op jit(solution)/shard_map/pallas_call | solution.py:541
  62.1 0.0 copy-start
  62.1 0.7 %copy-done = bf16[192,1024]{1,0:T(8,128)(2,1)} copy-done((bf16[192,1024]{1,0:T(8,128)(2,1)}, bf16[192,1024]{1,0:T(8,128)(2,1)S(1)}, u32[]{:S(2)}) %copy-start) | copy-done | bytes 393240
  62.8 0.0 copy-start.1
  62.8 0.8 %copy-done.1 = bf16[192,1024]{1,0:T(8,128)(2,1)} copy-done((bf16[192,1024]{1,0:T(8,128)(2,1)}, bf16[192,1024]{1,0:T(8,128)(2,1)S(1)}, u32[]{:S(2)}) %copy-start.1) | copy-done | bytes 393240
  63.6 0.0 copy-start.2
  63.6 0.6 copy-done.2
  64.2 2.1 %shard_map.77 = (bf16[192,1024]{1,0:T(8,128)(2,1)}, bf16[192,1024]{1,0:T(8,128)(2,1)}, f32[8,512]{1,0:T(8,128)}) custom-call(bf16[192,1024]{1,0:T(8,128)(2,1)} %copy-done, bf16[192,1024]{1,0:T(8,128)(2,1)} %copy-done.1, f32[8,512]{1,0:T(8,128)} %copy-done.2), custom_call_target="tpu_custom_call" | custom-call | tf_op jit(solution)/shard_map/pallas_call | solution.py:590
Async XLA Ops:
  62.1 0.7 %copy-start = (bf16[192,1024]{1,0:T(8,128)(2,1)}, bf16[192,1024]{1,0:T(8,128)(2,1)S(1)}, u32[]{:S(2)}) copy-start(bf16[192,1024]{1,0:T(8,128)(2,1)S(1)} %get-tuple-element.9.refs_0_) | copy-start | bytes 1179652
  62.8 0.8 %copy-start.1 = (bf16[192,1024]{1,0:T(8,128)(2,1)}, bf16[192,1024]{1,0:T(8,128)(2,1)S(1)}, u32[]{:S(2)}) copy-start(bf16[192,1024]{1,0:T(8,128)(2,1)S(1)} %get-tuple-element.10.refs_1_) | copy-start | bytes 1179652
  63.6 0.6 copy-start.2

commit v8 on v7

--- a/solution.py
+++ b/solution.py
@@ -85,7 +85,7 @@
     col_peers = [(dp, at, inner) for at in col_at]
     dp_peers = [
         (s, flip, (lax.rem(dp + s, n_dp), outer, x * 2 + (1 - core if flip else core)))
-        for s in range(n_dp)
+        for s in sorted(range(n_dp), key=lambda s: -min(s, n_dp - s))
         for flip in (0, 1)
         if s or flip
     ]
@@ -465,23 +465,28 @@
         mine[1, g] = share[8:]
 
     finish_kv(0)
+    row_first(0)
+    finish_kv(1)
+    row_first(1)
+    row_last(0)
+    row_last(1)
+
     for g in range(GROUPS):
         for b in range(2):
             rows = jnp.transpose(grad_query[g, b]) * FACTOR
             for m in range(2):
                 h = g * PER_GROUP + 2 * b + m
                 dq_out[:, h * HEAD : (h + 1) * HEAD] = rows[m * TOK : (m + 1) * TOK].astype(BF16)
-    row_first(0)
-    finish_kv(1)
-    row_first(1)
-    row_last(0)
     for g in range(GROUPS):
         swap[g].wait_recv()
     kv_rows = jnp.concatenate(
         [kv_own[kind, g] for kind in range(2) for g in range(GROUPS)], axis=1
     )
     dx_out[...] = product(kv_rows, weight[...], 1, 1).astype(BF16)
-    row_last(1)
+    others = [to_sibling(far_whole, g) for g in range(GROUPS)] + sib[1] + sib[3]
+    by_kind = [copy for group in far + near for kinds in group for copy in kinds]
+    for copy in halo + others + by_kind + here + swap + [rows_copy] + sum(row, []):
+        copy.wait_send()
     col_last(0)
     col_last(1)
 
@@ -494,6 +499,8 @@
         copy.start()
         last.append(copy)
     dp_buf[dp, core] = mine[core]
+    for copy in sum(col, []):
+        copy.wait_send()
     for copy in last:
         copy.wait_recv()
     for kind in range(2):
@@ -503,10 +510,7 @@
         for g in range(GROUPS):
             at = kind * GROUPS + g
             gw_ref[:, at * HEAD : (at + 1) * HEAD] = whole[g]
-
-    others = [to_sibling(far_whole, g) for g in range(GROUPS)] + sib[1] + sib[3]
-    by_kind = [copy for group in far + near for kinds in group for copy in kinds]
-    for copy in halo + others + by_kind + here + swap + [rows_copy] + sum(row + col, []) + last:
+    for copy in last:
         copy.wait_send()
 
 

time: 66.4 us -> 66.5 us (level)
  no operation moved by 1% of the time
where the time goes in v8:
time: 66.5 us; the launch traced here: 66.3 us
  Pallas kernels  63.6 us (96%)
  local copies, waits for them, and re-layouts  2.09 us (3%)
    pallas_call x1, Pallas kernels, on_device(): pl.pallas_call(functools.partial(kernel, *sizes), out_shape=tuple((pltpu....  61.5 us
    unnamed x6, local copies, waits for them, and re-layouts  2.09 us
    pallas_call x1, Pallas kernels, on_device(): pl.pallas_call(place, out_shape=shapes, in_specs=[inside] * 3, out_specs=...  2.06 us

profile of v8, /device:TPU:1, one launch (start us, length us, event | category | flops | bytes accessed | tf_op | source)
XLA Modules:
  0.0 66.3 jit_solution(7111731451726849817)
XLA Ops:
  0.6 61.5 %shard_map.76 = (bf16[192,1024]{1,0:T(8,128)(2,1)S(1)}, bf16[192,1024]{1,0:T(8,128)(2,1)S(1)}, f32[8,512]{1,0:T(8,128)S(1)}) custom-call(bf16[192,1024]{1,0:T(8,128)(2,1)} %bitcast.5, bf16[192,1024]{1,0:T(8,128)(2,1)} %bitcast.6, bf16[1024,512]{1,0:T(8,128)(2,1)} %w_hbm.1, bf16[192,1024]{1,0:T(8,128)(2,1)} %bitcast.7, s32[1,192]{1,0:T(1,128)} %ids_ref.1), custom_call_target="tpu_custom_call" | custom-call | tf_op jit(solution)/shard_map/pallas_call | solution.py:545
  62.1 0.0 copy-start
  62.1 0.7 %copy-done = bf16[192,1024]{1,0:T(8,128)(2,1)} copy-done((bf16[192,1024]{1,0:T(8,128)(2,1)}, bf16[192,1024]{1,0:T(8,128)(2,1)S(1)}, u32[]{:S(2)}) %copy-start) | copy-done | bytes 393240
  62.9 0.0 copy-start.1
  62.9 0.8 %copy-done.1 = bf16[192,1024]{1,0:T(8,128)(2,1)} copy-done((bf16[192,1024]{1,0:T(8,128)(2,1)}, bf16[192,1024]{1,0:T(8,128)(2,1)S(1)}, u32[]{:S(2)}) %copy-start.1) | copy-done | bytes 393240
  63.6 0.0 copy-start.2
  63.6 0.6 copy-done.2
  64.2 2.1 %shard_map.77 = (bf16[192,1024]{1,0:T(8,128)(2,1)}, bf16[192,1024]{1,0:T(8,128)(2,1)}, f32[8,512]{1,0:T(8,128)}) custom-call(bf16[192,1024]{1,0:T(8,128)(2,1)} %copy-done, bf16[192,1024]{1,0:T(8,128)(2,1)} %copy-done.1, f32[8,512]{1,0:T(8,128)} %copy-done.2), custom_call_target="tpu_custom_call" | custom-call | tf_op jit(solution)/shard_map/pallas_call | solution.py:594
Async XLA Ops:
  62.1 0.7 %copy-start = (bf16[192,1024]{1,0:T(8,128)(2,1)}, bf16[192,1024]{1,0:T(8,128)(2,1)S(1)}, u32[]{:S(2)}) copy-start(bf16[192,1024]{1,0:T(8,128)(2,1)S(1)} %get-tuple-element.9.refs_0_) | copy-start | bytes 1179652
  62.9 0.8 %copy-start.1 = (bf16[192,1024]{1,0:T(8,128)(2,1)}, bf16[192,1024]{1,0:T(8,128)(2,1)S(1)}, u32[]{:S(2)}) copy-start(bf16[192,1024]{1,0:T(8,128)(2,1)S(1)} %get-tuple-element.10.refs_1_) | copy-start | bytes 1179652
  63.6 0.6 copy-start.2

commit v9 on v8

--- a/solution.py
+++ b/solution.py
@@ -115,10 +115,8 @@
     ).astype(BF16)
     ids_query[...] = jnp.broadcast_to(twice[:, :PAIR], (8, PAIR))
 
-    pl.semaphore_wait(barrier, len(peers))
     loads[0].wait()
     rows_copy = remote(rows_in, rows_sib, rows_send, rows_recv, sibling)
-    rows_copy.start()
     far_whole, far_half = 4 * core, 4 * (1 - core)
 
     halo = []
@@ -150,8 +148,12 @@
             [weight[:, at : at + HEAD] for at in blocks[2 * g : 2 * g + 2]], axis=1
         )
         window[HERE, 0, g, 0:TOK, :] = product(rows_in[...], columns, 1, 0).astype(BF16)
+        if not g:
+            pl.semaphore_wait(barrier, len(peers))
         for i in (1, 2, 0):
             halo[8 * g + i].start()
+        if not g:
+            rows_copy.start()
 
     loads[5].wait()
     loads[6].wait()
@@ -388,8 +390,8 @@
     distant(1)
     send_whole(1)
     second_pass(far_half, 1, False, False)
+    send_half(1)
     second_and_send(1, 0)
-    send_half(1)
     second_and_send(3, 0)
     second_and_send(1, 1)
     send_near(0)

time: 66.5 us -> 66.7 us (level)
  no operation moved by 1% of the time
where the time goes in v9:
time: 66.7 us; the launch traced here: 66.5 us
  Pallas kernels  63.8 us (96%)
  local copies, waits for them, and re-layouts  2.09 us (3%)
    pallas_call x1, Pallas kernels, on_device(): pl.pallas_call(functools.partial(kernel, *sizes), out_shape=tuple((pltpu....  61.7 us
    unnamed x6, local copies, waits for them, and re-layouts  2.09 us
    pallas_call x1, Pallas kernels, on_device(): pl.pallas_call(place, out_shape=shapes, in_specs=[inside] * 3, out_specs=...  2.06 us

profile of v9, /device:TPU:1, one launch (start us, length us, event | category | flops | bytes accessed | tf_op | source)
XLA Modules:
  0.0 66.5 jit_solution(15597188103745973063)
XLA Ops:
  0.6 61.7 %shard_map.76 = (bf16[192,1024]{1,0:T(8,128)(2,1)S(1)}, bf16[192,1024]{1,0:T(8,128)(2,1)S(1)}, f32[8,512]{1,0:T(8,128)S(1)}) custom-call(bf16[192,1024]{1,0:T(8,128)(2,1)} %bitcast.5, bf16[192,1024]{1,0:T(8,128)(2,1)} %bitcast.6, bf16[1024,512]{1,0:T(8,128)(2,1)} %w_hbm.1, bf16[192,1024]{1,0:T(8,128)(2,1)} %bitcast.7, s32[1,192]{1,0:T(1,128)} %ids_ref.1), custom_call_target="tpu_custom_call" | custom-call | tf_op jit(solution)/shard_map/pallas_call | solution.py:547
  62.4 0.0 copy-start
  62.4 0.7 %copy-done = bf16[192,1024]{1,0:T(8,128)(2,1)} copy-done((bf16[192,1024]{1,0:T(8,128)(2,1)}, bf16[192,1024]{1,0:T(8,128)(2,1)S(1)}, u32[]{:S(2)}) %copy-start) | copy-done | bytes 393240
  63.1 0.0 copy-start.1
  63.1 0.8 %copy-done.1 = bf16[192,1024]{1,0:T(8,128)(2,1)} copy-done((bf16[192,1024]{1,0:T(8,128)(2,1)}, bf16[192,1024]{1,0:T(8,128)(2,1)S(1)}, u32[]{:S(2)}) %copy-start.1) | copy-done | bytes 393240
  63.9 0.0 copy-start.2
  63.9 0.6 copy-done.2
  64.5 2.1 %shard_map.77 = (bf16[192,1024]{1,0:T(8,128)(2,1)}, bf16[192,1024]{1,0:T(8,128)(2,1)}, f32[8,512]{1,0:T(8,128)}) custom-call(bf16[192,1024]{1,0:T(8,128)(2,1)} %copy-done, bf16[192,1024]{1,0:T(8,128)(2,1)} %copy-done.1, f32[8,512]{1,0:T(8,128)} %copy-done.2), custom_call_target="tpu_custom_call" | custom-call | tf_op jit(solution)/shard_map/pallas_call | solution.py:596
Async XLA Ops:
  62.4 0.7 %copy-start = (bf16[192,1024]{1,0:T(8,128)(2,1)}, bf16[192,1024]{1,0:T(8,128)(2,1)S(1)}, u32[]{:S(2)}) copy-start(bf16[192,1024]{1,0:T(8,128)(2,1)S(1)} %get-tuple-element.9.refs_0_) | copy-start | bytes 1179652
  63.1 0.8 %copy-start.1 = (bf16[192,1024]{1,0:T(8,128)(2,1)}, bf16[192,1024]{1,0:T(8,128)(2,1)S(1)}, u32[]{:S(2)}) copy-start(bf16[192,1024]{1,0:T(8,128)(2,1)S(1)} %get-tuple-element.10.refs_1_) | copy-start | bytes 1179652
  63.9 0.6 copy-start.2
